TPU v7x, 256 devices: a whole 4x4x8 slice. The times are simulated.
256 devices in a mesh: loop: 16 (over x_hi, z), column: 4 (over y), dp: 4 (over x_lo, core).
Axes of the slice: x: 4 (x_hi: 2, x_lo: 2; x = x_hi * 2 + x_lo), y: 4, z: 8, core: 2. Of those that a mesh axis runs over, the one named last changes fastest.
Arguments:
- tokens: bfloat16 [4096, 16384], P('dp', 'loop'), may hold values from -8 to 8
- doc_ids: int32 [4096], P('dp'), may hold values from 0 to 11, never falling along the last dimension, each value on 1 to 1536 neighbouring positions
- w_query: bfloat16 [16384, 8192], P('loop', 'column'), may hold values from -1.00581 to 1.00581
- key_weight: bfloat16 [16384, 512], P('loop', 'column'), may hold values from -0.0390625 to 0.0390625
- value_weight: bfloat16 [16384, 512], P('loop', 'column'), may hold values from -0.046875 to 0.046875
- w_out: bfloat16 [8192, 16384], P('column', 'loop'), may hold values from -0.09375 to 0.09375
Outputs:
- result: bfloat16 [4096, 16384], P('dp', ('loop', 'column'))
Inputs may be any that keep to these rules, and one draw needn't show every extreme that they name: `doc_ids`: never falling along the tokens; each document spans 1 to 1536 tokens and one spans exactly that many.
All inputs are finite; a program needn't handle non-finite values.
Results may differ from a plain program's by a relative error of at most 0.0078.
Values may be sent and summed in bfloat16 or wider, within the bound.
A program may use at most 64 MiB of HBM per device.

v0:
```python
import jax
import jax.numpy as jnp
from jax import lax
from jax.sharding import PartitionSpec as P

HEAD_SIZE = 128
SEQUENCE_TOKENS = 1024


def rotate(vectors, positions):
    half_width = vectors.shape[-1] // 2
    frequency = jnp.exp(
        -jnp.log(500000.0) * jnp.arange(half_width, dtype=jnp.float32) * 2.0 / vectors.shape[-1]
    )
    angles = positions.astype(jnp.float32)[:, None, None] * frequency
    cosine = jnp.cos(angles)
    sine_table = jnp.sin(angles)
    leading = vectors[..., :half_width]
    trailing = vectors[..., half_width:]
    return jnp.concatenate(
        [leading * cosine - trailing * sine_table, trailing * cosine + leading * sine_table], -1
    )


def shards(tokens, doc_ids, w_query, key_weight, value_weight, w_out):
    group_rows = tokens.shape[0]
    loop_count = lax.axis_size("loop")
    loop_index = lax.axis_index("loop")
    slab_rows = group_rows // loop_count
    query_cols = w_query.shape[1]
    kv_cols = key_weight.shape[1]
    local_heads = query_cols // HEAD_SIZE
    local_kv = kv_cols // HEAD_SIZE
    queries_per_group = local_heads // local_kv
    first_local = loop_index * slab_rows
    query_order = first_local + jnp.arange(slab_rows, dtype=jnp.int32)
    summed = lax.psum_scatter(
        jnp.concatenate(
            [
                jnp.dot(tokens, w_query, preferred_element_type=jnp.float32),
                jnp.dot(tokens, key_weight, preferred_element_type=jnp.float32),
                jnp.dot(tokens, value_weight, preferred_element_type=jnp.float32),
            ],
            1,
        ),
        "loop",
        scatter_dimension=0,
        tiled=True,
    )
    raw_query = summed[:, :query_cols].reshape(slab_rows, local_heads, HEAD_SIZE)
    unprojected_key = summed[:, query_cols : query_cols + kv_cols].reshape(
        slab_rows, local_kv, HEAD_SIZE
    )
    unprojected_value = summed[:, query_cols + kv_cols :].reshape(slab_rows, local_kv, HEAD_SIZE)
    key = rotate(unprojected_key, query_order % SEQUENCE_TOKENS).astype(jnp.bfloat16)
    value = unprojected_value.astype(jnp.bfloat16)
    query_matrix = rotate(raw_query, query_order % SEQUENCE_TOKENS).astype(jnp.bfloat16)
    query_groups = query_matrix.reshape(slab_rows, local_kv, queries_per_group, HEAD_SIZE)
    query_docs = lax.dynamic_slice_in_dim(doc_ids, first_local, slab_rows, 0)
    scale = 1.0 / HEAD_SIZE**0.5
    start_max = jnp.full((local_kv, queries_per_group, slab_rows), -1e30, jnp.float32)
    key_piece = lax.all_gather(key, "loop", axis=0, tiled=True)
    value_piece = lax.all_gather(value, "loop", axis=0, tiled=True)
    row_count = key_piece.shape[0]
    key_order = jnp.arange(row_count, dtype=jnp.int32)
    allowed = (query_docs[:, None] == doc_ids[None, :]) & (
        key_order[None, :] <= query_order[:, None]
    )
    scores = (
        jnp.einsum("qkgd,pkd->kgqp", query_groups, key_piece, preferred_element_type=jnp.float32)
        * scale
    )
    masked = jnp.where(allowed, scores, -1e30)
    new_max = jnp.maximum(start_max, jnp.max(masked, axis=-1))
    weights = jnp.where(allowed, jnp.exp(masked - new_max[..., None]), 0.0)
    denominator = jnp.sum(weights, axis=-1)
    accum = jnp.einsum("kgqp,pkd->kgqd", weights, value_piece.astype(jnp.float32))
    final_max, denominator, accum = (new_max, denominator, accum)
    attended = accum / denominator[..., None]
    attended = (
        jnp.transpose(attended, (2, 0, 1, 3)).reshape(slab_rows, query_cols).astype(jnp.bfloat16)
    )
    partial_out = jnp.dot(
        lax.all_gather(attended, "loop", axis=0, tiled=True),
        w_out,
        preferred_element_type=jnp.float32,
    )
    return lax.psum_scatter(partial_out, "column", scatter_dimension=1, tiled=True).astype(
        jnp.bfloat16
    )


def solution(mesh):
    placed = (
        P("dp", "loop"),
        P("dp"),
        P("loop", "column"),
        P("loop", "column"),
        P("loop", "column"),
        P("column", "loop"),
    )
    return jax.shard_map(
        shards, mesh=mesh, in_specs=placed, out_specs=P("dp", ("loop", "column")), check_vma=False
    )
```

profile of v0, /device:TPU:2, one launch (start us, length us, event | category | flops | bytes accessed | tf_op | source)
XLA Modules:
  0.0 501.7 jit_solution(12117867909786246871)
XLA Ops:
  6.5 0.0 copy-start
  6.5 0.0 reduce-scatter.3.cloned.1.call-start
  6.5 1.6 copy-done
  8.1 0.0 copy-start.2
  8.1 1.8 fusion.42
  9.9 1.7 fusion.41
  11.6 0.0 copy-done.2
  11.6 4.5 fusion.40
  16.1 4.4 pad_maximum_fusion
  20.5 0.0 copy-start.1
  20.5 0.0 reduce-scatter.3.cloned.1.call-update
  20.5 0.0 all-gather.3.cloned.1.call-start
  20.6 0.6 copy-done.1
  21.2 0.1 dynamic_slice.3
  21.3 0.2 multiply_cosine_fusion
  21.5 0.1 fusion.24
  21.6 233.4 %reduce-scatter.3.cloned.1.call-done = f32[64,2304]{1,0:T(8,128)} async-done(((f32[1024,2304]{1,0:T(8,128)}), f32[64,2304]{1,0:T(8,128)}) %reduce-scatter.3.cloned.1.call-update) | async-done | bytes 589840 | tf_op jit(solution)/shard_map/reduce_scatter | solution.py:37
  255.1 1.1 slice_bitcast_fusion
  256.1 0.1 copy.20
  256.2 0.2 fusion.39
  256.4 0.8 slice_bitcast_fusion.1
  257.2 0.2 fusion.30
  257.4 0.1 pad_maximum_fusion.1
  257.5 39.9 %all_gather.9 = bf16[1024,1,128]{2,0,1:T(8,128)(2,1)S(1)} all-gather(bf16[64,1,128]{2,0,1:T(8,128)(2,1)S(1)} %pad_maximum_fusion.1), channel_id=1, replica_groups=mesh['loop'=16,'column'=4,'dp'=4] {'loop'}, dimensions={0}, use_global_device_ids=true | all-gather | bytes 278528 | tf_op jit(solution)/shard_map/all_gather | solution.py:62
  297.4 0.4 subtract_convert_fusion
  297.7 1.0 fusion.2
  298.7 0.8 slice.43
  299.5 36.9 %all-gather = bf16[1024,128]{1,0:T(8,128)(2,1)S(1)} all-gather(bf16[64,128]{1,0:T(8,128)(2,1)S(1)} %slice.43), channel_id=2, replica_groups=mesh['loop'=16,'column'=4,'dp'=4] {'loop'}, dimensions={0}, use_global_device_ids=true | all-gather | bytes 278528 | tf_op jit(solution)/shard_map/all_gather | solution.py:63
  336.4 1.3 fusion.3
  337.7 1.2 fusion.15
  338.9 0.2 copy.15
  339.1 0.8 copy.27
  339.9 0.0 all-gather.3.cloned.1.call-update
  339.9 0.2 reduce-scatter.5.cloned.1.call-start
  340.1 96.1 %all-gather.3.cloned.1.call-done = bf16[1024,2048]{1,0:T(8,128)(2,1)} async-done(((bf16[64,2048]{1,0:T(8,128)(2,1)}), bf16[1024,2048]{1,0:T(8,128)(2,1)}) %all-gather.3.cloned.1.call-update) | async-done | bytes 4194320 | tf_op jit(solution)/shard_map/all_gather | solution.py:84
  436.3 9.9 %fusion.43 = f32[1024,1024]{1,0:T(8,128)} fusion(bf16[1024,2048]{1,0:T(8,128)(2,1)} %all-gather.3.cloned.1.call-done, bf16[2048,1024]{1,0:T(8,128)(2,1)} %param.11), kind=kOutput, calls=%fused_computation.58 | convolution fusion | flops 4294967296 | bytes 12582912 | tf_op jit(solution)/shard_map/dot_general | solution.py:83
  446.1 0.0 reduce-scatter.5.cloned.1.call-update
  446.2 47.0 %reduce-scatter.5.cloned.1.call-done = f32[1024,256]{1,0:T(8,128)} async-done(((f32[1024,1024]{1,0:T(8,128)}), f32[1024,256]{1,0:T(8,128)}) %reduce-scatter.5.cloned.1.call-update) | async-done | bytes 1048592 | tf_op jit(solution)/shard_map/reduce_scatter | solution.py:88
  493.1 2.1 convert_element_type.46
  (4 shorter events, 0.0 us)
Async XLA Ops:
  6.5 1.6 copy-start
  6.5 248.5 %reduce-scatter.3.cloned.1.call-start = ((), (), s32[]{:S(2)}) async-start(), calls=%async_computation.2 | async-start | bytes 10027008 | tf_op jit(solution)/shard_map/reduce_scatter | solution.py:37
  8.1 3.5 copy-start.2
  20.5 0.7 copy-start.1
  20.5 415.7 %all-gather.3.cloned.1.call-start = ((), (), s32[]{:S(2)}) async-start(), calls=%async_computation.3 | async-start | bytes 4456448 | tf_op jit(solution)/shard_map/all_gather | solution.py:84
  339.9 153.2 %reduce-scatter.5.cloned.1.call-start = ((), (), s32[]{:S(2)}) async-start(), calls=%async_computation.4 | async-start | bytes 5242880 | tf_op jit(solution)/shard_map/reduce_scatter | solution.py:88
Sparse Core Ops, SparseCore 0:
  20.6 234.3 reduce-scatter.2
  340.0 96.2 all-gather.2
  446.3 46.7 reduce-scatter.4
where the time goes:
time: 503 us; the launch traced here: 502 us
  waiting for transfers between devices  377 us (75%)
  blocking collectives  76.8 us (15%)
  matrix products  20 us (4%)
  between operations  13.2 us (3%)
  other arithmetic  8.78 us (2%)
  local copies, waits for them, and re-layouts  6.12 us (1%)
    reduce_scatter x1, waiting for transfers between devices, shards(): lax.psum_scatter(jnp.concatenate([jnp.dot(tokens, w_query, preferred_elem...  233 us
    all_gather x1, waiting for transfers between devices, shards(): lax.all_gather(attended, 'loop', axis=0, tiled=True)  96.1 us
    reduce_scatter x1, waiting for transfers between devices, shards(): lax.psum_scatter(partial_out, 'column', scatter_dimension=1, tiled=True)  47 us
    all_gather x1, blocking collectives, shards(): key_piece = lax.all_gather(key, 'loop', axis=0, tiled=True)  39.9 us
    all_gather x1, blocking collectives, shards(): value_piece = lax.all_gather(value, 'loop', axis=0, tiled=True)  36.9 us
  transfers between devices with their start and end apart: 3, of which 3 were waited for; matrix products, arithmetic and copies ran while one was open for 0% of the time, Pallas kernels for 0%

commit v1 on v0

v1 whole, which is shorter than its diff:
```python
import functools
import math

import jax
import jax.numpy as jnp
import numpy as np
from jax import lax
from jax.experimental import pallas as pl
from jax.experimental.pallas import tpu as pltpu
from jax.sharding import PartitionSpec as P

HEAD = 128
SEQ = 1024
MODEL = 1024
QCOLS = 2048
OCOLS = 1024
NZ = 8
NY = 4
CHUNKS = 2
ROWS = SEQ // CHUNKS
R = ROWS // (2 * NZ)
XFIRST = ((0, 640), (640, 640))
ZFIRST = ((1280, 384), (1664, 384))
BF = jnp.bfloat16
F32 = jnp.float32
SCALE = math.log2(math.e) / math.sqrt(HEAD)
ORDER = (
    0, 13, 21, 9, 5, 18, 1, 148, 45, 152, 4, 82, 79, 14, 75, 10, 3, 19, 22, 60, 46, 149, 76, 81, 2, 53, 59, 153,
    80, 11, 78, 64, 6, 157, 41, 7, 160, 77, 63, 61, 23, 15, 65, 83, 12, 150, 54, 50, 42, 24, 86, 16, 62, 158, 161,
    91, 66, 67, 55, 8, 47, 20, 43, 182, 17, 87, 189, 151, 71, 183, 68, 187, 56, 27, 30, 159, 162, 25, 51, 154, 167,
    188, 184, 166, 84, 44, 31, 26, 69, 88, 28, 72, 186, 185, 193, 32, 85, 169, 34, 170, 163, 173, 171, 70, 38, 155,
    168, 48, 190, 73, 33, 29, 172, 52, 177, 194, 89, 174, 35, 39, 74, 191, 94, 178, 57, 175, 195, 36, 90, 114, 95,
    127, 110, 49, 124, 92, 198, 179, 58, 196, 192, 40, 37, 164, 93, 111, 115, 125, 128, 134, 180, 100, 117, 96,
    121, 165, 106, 176, 156, 200, 103, 116, 131, 197, 202, 199, 122, 231, 234, 129, 112, 181, 201, 97, 220, 101,
    135, 217, 232, 104, 107, 210, 126, 113, 118, 132, 140, 203, 238, 235, 221, 123, 245, 218, 241, 207, 102, 227,
    119, 233, 224, 213, 142, 108, 222, 130, 136, 236, 138, 246, 208, 105, 228, 98, 133, 219, 214, 239, 247, 242,
    240, 204, 211, 223, 225, 137, 109, 99, 144, 141, 237, 120, 215, 209, 205, 243, 226, 212, 143, 229, 249, 146,
    230, 248, 216, 206, 244, 251, 253, 250, 147, 145, 252, 139, 254,
)


def narrow(value):
    return value.astype(BF)


def widen(value):
    return value.astype(F32)


def narrow_pair(value):
    key = value[..., 0:HEAD]
    high = key.astype(BF)
    low = (key - high.astype(F32)).astype(BF)
    return jnp.concatenate([high, low, value[..., HEAD : 2 * HEAD].astype(BF)], -1)


def widen_pair(value):
    value = value.astype(F32)
    key = value[..., 0:HEAD] + value[..., HEAD : 2 * HEAD]
    return jnp.concatenate([key, value[..., 2 * HEAD : 3 * HEAD]], -1)


class Node:
    def __init__(self, name, rank, cost, after, waits, sends, emit):
        self.name, self.rank, self.cost = name, rank, cost
        self.after, self.waits, self.sends, self.emit = after, waits, sends, emit


def rotary_table():
    frequency = np.exp(-np.log(500000.0) * np.arange(HEAD // 2, dtype=np.float64) * 2.0 / HEAD)
    angles = np.arange(SEQ, dtype=np.float64)[:, None] * frequency
    cosine, sine = np.cos(angles), np.sin(angles)
    table = np.concatenate([cosine, cosine, -sine, sine], 1).astype(np.float32)
    return table.reshape(CHUNKS, 2 * NZ, R, 2 * HEAD)


def split(parity):
    return (4, 3) if parity == 0 else (3, 4)


def build(k):
    nodes = []

    def add(name, rank, cost, after, waits, sends, emit):
        nodes.append(Node(name, rank, cost, after, waits, sends, emit))

    def zlink(sign):
        return ["z+"] if sign > 0 else ["z-"]

    def emit_kv():
        k.load("wkv")
        for t in range(CHUNKS):
            k.load("tok%d" % t)
            res = jnp.dot(k.tok[pl.ds(t * ROWS, ROWS)], k.wkv[...], preferred_element_type=F32)
            k.pkv[t] = res.reshape(NZ, 2, R, 2 * HEAD)
        k.ready()

    add("kvmm", 0, 3.0, [], [], [], emit_kv)

    def emit_q(t, c0, width):
        k.load("tok%d" % t)
        for c in range(c0 // 512, (c0 + width - 1) // 512 + 1):
            k.load("wq%d" % c)
        res = jnp.dot(k.tok[pl.ds(t * ROWS, ROWS)], k.wq[:, c0 : c0 + width], preferred_element_type=F32)
        k.pq[t, :, :, :, c0 : c0 + width] = res.reshape(NZ, 2, R, width)

    for t in range(CHUNKS):
        for c0, width in ZFIRST + XFIRST:
            add(
                "q%d_%d" % (t, c0),
                1 + t * 40 + (0.1 if c0 < ZFIRST[0][0] else 0),
                width / 600.0,
                ["kvmm"],
                [],
                [],
                functools.partial(emit_q, t, c0, width),
            )

    def ring(tag, rank, stride, cost, size, counts, own, start_after, step_waits, down=narrow, up=widen):
        for sign, n in ((1, counts[0]), (-1, counts[1])):
            base = 0 if sign > 0 else counts[0]
            for s in range(n):
                name = (tag, sign, s)

                def emit(sign=sign, n=n, s=s, base=base, name=name):
                    d = k.zi(sign * (n - s))
                    value = own(sign, s, d)
                    if s > 0:
                        value = value + up(k.buf[tag, "r"][base + s - 1])
                    k.buf[tag, "s"][base + s] = down(value)
                    k.send(name, k.buf[tag, "s"].at[base + s], k.buf[tag, "r"].at[base + s], k.dev_z(sign))

                waits = list(step_waits(sign, s))
                after = list(start_after)
                if s > 0:
                    waits.append((tag, sign, s - 1))
                    after.append((tag, sign, s - 1))
                add(name, rank + stride * s, cost, after, waits, [(name, zlink(sign), size)], emit)
        return [(tag, 1, counts[0] - 1), (tag, -1, counts[1] - 1)]

    def ring_sum(tag, counts, pick, up=widen):
        bufs = k.buf[tag, "r"]
        return up(pick(bufs, counts[0] - 1)) + up(pick(bufs, NZ - 2))

    for t in range(CHUNKS):
        tag, counts, base = "kv%d" % t, split(t), 20 * t
        last = ring(
            tag,
            base + 2,
            4,
            0.15,
            2 * R * 768,
            counts,
            lambda sign, s, d, t=t: k.pkv[t, d],
            ["kvmm"],
            lambda sign, s: [],
            narrow_pair,
            widen_pair,
        )

        def emit_kv_fin(t=t, tag=tag, counts=counts):
            o = 1 - k.xh
            value = k.pkv[t, k.z, o] + ring_sum(tag, counts, lambda b, i: b[i, o], widen_pair)
            k.buf[tag + "x", "s"][...] = narrow_pair(value)
            k.send(tag + "x", k.buf[tag + "x", "s"], k.buf[tag + "x", "r"], k.dev_x())

        add(tag + "fin", base + 2, 0.12, last, last, [(tag + "x", ["x"], R * 768)], emit_kv_fin)

        def emit_kv_own(t=t, tag=tag, counts=counts):
            k.load("tab")
            value = k.pkv[t, k.z, k.xh] + ring_sum(tag, counts, lambda b, i: b[i, k.xh], widen_pair)
            value = value + widen_pair(k.buf[tag + "x", "r"][...])
            k.kvf[t, k.z, k.xh, :, 0:HEAD] = k.rotate(value[:, 0:HEAD], t).astype(BF)
            k.kvf[t, k.z, k.xh, :, HEAD : 2 * HEAD] = value[:, HEAD : 2 * HEAD].astype(BF)
            here = k.kvf.at[t, k.z, k.xh]
            k.send("kgx%d" % t, here, here, k.dev_x())

        add(tag + "own", base + 2, 0.2, [tag + "fin"], [tag + "x"], [("kgx%d" % t, ["x"], R * 512)], emit_kv_own)

    def gather(tag, rank, stride, size, counts, block, start_after, start_waits):
        for sign, n in ((1, counts[0]), (-1, counts[1])):
            for s in range(n):
                name = (tag, sign, s)

                def emit(sign=sign, s=s, name=name):
                    here = block(k.zi(-sign * s))
                    k.send(name, here, here, k.dev_z(sign))

                after = list(start_after) if s == 0 else [(tag, sign, s - 1)]
                waits = list(start_waits) if s == 0 else [(tag, sign, s - 1)]
                add(name, rank + stride * s, 0.05, after, waits, [(name, zlink(sign), size)], emit)
        return [(tag, 1, counts[0] - 1), (tag, -1, counts[1] - 1)]

    kg_last = [
        gather(
            "kg%d" % t,
            20 * t + 2,
            1,
            2 * R * 512,
            split(1 - t),
            lambda d, t=t: k.kvf.at[t, d],
            ["kv%down" % t],
            ["kgx%d" % t],
        )
        for t in range(CHUNKS)
    ]

    for t in range(CHUNKS):
        base = 40 * t
        own_nodes = {}
        for j, (c0, width) in enumerate(ZFIRST):
            tag, counts = "zf%d_%d" % (t, c0), split(j)
            last = ring(
                tag,
                base + 3 + 0.2 * j,
                8,
                0.15,
                2 * R * width * 2,
                counts,
                lambda sign, s, d, c0=c0, width=width, t=t: k.pq[t, d, :, :, c0 : c0 + width],
                ["q%d_%d" % (t, c0)],
                lambda sign, s: [],
            )

            def emit_fin(t=t, tag=tag, c0=c0, width=width, counts=counts):
                o = 1 - k.xh
                value = k.pq[t, k.z, o, :, c0 : c0 + width] + ring_sum(tag, counts, lambda b, i: b[i, o])
                k.buf[tag + "x", "s"][...] = value.astype(BF)
                k.send(tag + "x", k.buf[tag + "x", "s"], k.buf[tag + "x", "r"], k.dev_x())

            add(tag + "fin", base + 36, 0.1, last, last, [(tag + "x", ["x"], R * width * 2)], emit_fin)

            def emit_own(t=t, tag=tag, c0=c0, width=width, counts=counts):
                k.load("tab")
                value = k.pq[t, k.z, k.xh, :, c0 : c0 + width] + ring_sum(tag, counts, lambda b, i: b[i, k.xh])
                k.store_query(t, c0, value + k.buf[tag + "x", "r"][...].astype(F32))

            add(tag + "own", base + 37, 0.15, [tag + "fin"], [tag + "x"], [], emit_own)
            own_nodes[c0] = tag + "own"

        for j, (c0, width) in enumerate(XFIRST):
            tag, counts = "xf%d_%d" % (t, c0), split(j + t)
            slots = [(1, s) for s in range(counts[0])] + [(-1, s) for s in range(counts[1])] + [(0, 0)]
            queue = sorted(range(NZ), key=lambda i, slots=slots: (slots[i][1] if slots[i][0] else 9, i))

            def where(i, counts=counts, slots=slots):
                sign, s = slots[i]
                n = counts[0] if sign > 0 else counts[1]
                return k.zi(sign * (n - s)) if sign else k.z

            for place, i in enumerate(queue):

                def emit_x(t=t, tag=tag, i=i, c0=c0, width=width, where=where):
                    k.buf[tag + "x", "s"][i] = k.pq[t, where(i), 1 - k.xh, :, c0 : c0 + width].astype(BF)
                    k.send((tag, "x", i), k.buf[tag + "x", "s"].at[i], k.buf[tag + "x", "r"].at[i], k.dev_x())

                add(
                    (tag, "x", i),
                    base + 4 + 0.1 * place - (8 if t else 0),
                    0.06,
                    ["q%d_%d" % (t, c0)],
                    [],
                    [((tag, "x", i), ["x"], R * width * 2)],
                    emit_x,
                )

            def own_xf(sign, s, d, t=t, tag=tag, c0=c0, width=width, counts=counts):
                i = s if sign > 0 else counts[0] + s
                return k.pq[t, d, k.xh, :, c0 : c0 + width] + k.buf[tag + "x", "r"][i].astype(F32)

            last = ring(
                tag,
                base + 9,
                8,
                0.15,
                R * width * 2,
                counts,
                own_xf,
                [(tag, "x", i) for i in range(NZ)],
                lambda sign, s, tag=tag, counts=counts: [(tag, "x", s if sign > 0 else counts[0] + s)],
            )

            def emit_xf_own(t=t, tag=tag, c0=c0, width=width, counts=counts):
                k.load("tab")
                value = k.pq[t, k.z, k.xh, :, c0 : c0 + width] + k.buf[tag + "x", "r"][NZ - 1].astype(F32)
                k.store_query(t, c0, value + ring_sum(tag, counts, lambda b, i: b[i]))

            add(tag + "own", base + 37.5, 0.15, last, last + [(tag, "x", NZ - 1)], [], emit_xf_own)
            own_nodes[c0] = tag + "own"

        add("mask%d" % t, base + 20, 0.3, ["kvmm"], [], [], functools.partial(lambda t: k.mask(t), t))
        keys_in = [m for u in range(t + 1) for m in ["kgx%d" % u] + kg_last[u]]
        keys_after = [m for u in range(t + 1) for m in ["kv%down" % u] + kg_last[u]]
        for place, (c0, width) in enumerate(ZFIRST + XFIRST):
            gtag = "g%d_%d" % (t, c0)

            def emit_att(t=t, gtag=gtag, c0=c0, width=width):
                k.attend(t, c0 // HEAD, width // HEAD)
                here = k.att.at[t, k.z, k.xh, :, c0 : c0 + width]
                k.send((gtag, "x", 0), here, here, k.dev_x())

            add(
                gtag + "att",
                base + 40 + place,
                width / 1000.0 + 0.05,
                [own_nodes[c0], "mask%d" % t] + keys_after,
                keys_in,
                [((gtag, "x", 0), ["x"], R * width * 2)],
                emit_att,
            )
        last_step = []
        for j, (c0, width) in enumerate(ZFIRST):
            gtag = "g%d_%d" % (t, c0)
            gather(
                gtag,
                base + 44 + 0.1 * j,
                4,
                2 * R * width * 2,
                split(j),
                lambda d, t=t, c0=c0, width=width: k.att.at[t, d, :, :, c0 : c0 + width],
                [gtag + "att"],
                [(gtag, "x", 0)],
            )
            last_step.append((gtag, False, split(j)))
        for j, (c0, width) in enumerate(XFIRST):
            gtag, counts = "g%d_%d" % (t, c0), split(j + t)
            gather(
                gtag,
                base + 43,
                4,
                R * width * 2,
                counts,
                lambda d, t=t, c0=c0, width=width: k.att.at[t, d, k.xh, :, c0 : c0 + width],
                [gtag + "att"],
                [],
            )
            last_step.append((gtag, True, counts))
            for sign, n in ((1, counts[0]), (-1, counts[1])):
                for s in range(n):
                    name = (gtag, "x", sign, s)

                    def emit_pass(t=t, sign=sign, s=s, name=name, c0=c0, width=width):
                        here = k.att.at[t, k.zi(-sign * (s + 1)), k.xh, :, c0 : c0 + width]
                        k.send(name, here, here, k.dev_x())

                    after = [(gtag, sign, s + 1)] if s + 1 < n else [(gtag, sign, s)]
                    add(
                        name,
                        base + 43.5 + 4 * s,
                        0.05,
                        after,
                        [(gtag, sign, s)],
                        [(name, ["x"], R * width * 2)],
                        emit_pass,
                    )
        for r in range(5):
            shifts = [0] if r == 0 else [4] if r == 4 else [-r, r]
            first = 0 if r == 0 else 2 * r - 1
            waits, after = [], []
            for gtag, passes, counts in last_step:
                if r == 0:
                    waits.append((gtag, "x", 0))
                    after.append(gtag + "att")
                for sign, n in ((1, counts[0]), (-1, counts[1])):
                    if 0 < r <= n:
                        waits.append((gtag, sign, r - 1))
                        after.append((gtag, sign, r - 1))
                        if passes:
                            waits.append((gtag, "x", sign, r - 1))
                            after.append((gtag, "x", sign, r - 1))

            def emit_out(t=t, r=r, shifts=shifts, first=first):
                k.load("wout")
                count = len(shifts)
                rows = [k.att[t, k.zi(s)].reshape(2 * R, QCOLS) for s in shifts]
                lhs = rows[0] if count == 1 else jnp.concatenate(rows, 0)
                for delta in (2, 1, 3, 0):
                    c0 = pl.multiple_of(lax.rem(k.y + delta, NY) * 256, 256)
                    res = jnp.dot(lhs, k.wout[:, pl.ds(c0, 256)], preferred_element_type=F32)
                    res = res.reshape(count, 2 * R, 256)
                    if delta == 0:
                        k.oown[t, first : first + count] = res
                    else:
                        k.ys[t, delta - 1, first : first + count] = res.astype(BF)
                        k.send(
                            ("y", t, r, delta),
                            k.ys.at[t, delta - 1, first : first + count],
                            k.yr.at[t, delta - 1, first : first + count],
                            k.dev_y(delta),
                        )

            size = len(shifts) * 2 * R * 512
            add(
                ("out", t, r),
                base + 45 + 4 * r,
                1.4,
                after,
                waits,
                [(("y", t, r, 2), ["y+", "y-"], size), (("y", t, r, 1), ["y+"], size), (("y", t, r, 3), ["y-"], size)],
                emit_out,
            )

            def emit_fin(t=t, shifts=shifts, first=first):
                for i, shift in enumerate(shifts):
                    total = k.oown[t, first + i]
                    for delta in range(NY - 1):
                        total = total + k.yr[t, delta, first + i].astype(F32)
                    row = pl.multiple_of(t * ROWS + k.zi(shift) * 2 * R, 2 * R)
                    k.out[pl.ds(row, 2 * R), :] = total.astype(BF)

            add(
                ("fin", t, r),
                base + 50 + 4 * r,
                0.15,
                [("out", t, r)],
                [("y", t, r, delta) for delta in (1, 2, 3)],
                [],
                emit_fin,
            )
    return nodes


def buffers():
    shapes = {}
    for t in range(CHUNKS):
        shapes["kv%d" % t] = (7, 2, R, 384)
        shapes["kv%dx" % t] = (R, 384)
        for c0, width in ZFIRST:
            shapes["zf%d_%d" % (t, c0)] = (7, 2, R, width)
            shapes["zf%d_%dx" % (t, c0)] = (R, width)
        for c0, width in XFIRST:
            shapes["xf%d_%d" % (t, c0)] = (7, R, width)
            shapes["xf%d_%dx" % (t, c0)] = (8, R, width)
    return shapes


class Kernel:
    pass


def kernel(order_names, messages, *refs):
    shapes = buffers()
    names = ["docs", "h_tok", "h_wq", "h_wk", "h_wv", "h_wout", "h_tab", "out"]
    names += ["tok", "wq", "wkv", "wout", "tab", "bias", "pq", "pkv", "kvf", "qs", "att", "oown", "ys", "yr"]
    k = Kernel()
    for name, ref in zip(names, refs):
        setattr(k, name, ref)
    rest = refs[len(names) :]
    k.buf = {}
    for i, name in enumerate(shapes):
        k.buf[name, "s"], k.buf[name, "r"] = rest[2 * i], rest[2 * i + 1]
    send_sem, recv_sem, load_sem = rest[2 * len(shapes) :]

    loop, k.y = lax.axis_index("loop"), lax.axis_index("column")
    k.xh, k.z = loop // NZ, lax.rem(loop, NZ)
    k.zi = lambda delta: lax.rem(k.z + (delta + NZ), NZ) if delta else k.z
    k.dev_z = lambda sign: {"loop": k.xh * NZ + k.zi(sign)}
    k.dev_x = lambda: {"loop": (1 - k.xh) * NZ + k.z}
    k.dev_y = lambda delta: {"column": lax.rem(k.y + delta, NY)}
    mesh_id = pl.DeviceIdType.MESH

    barrier = pltpu.get_barrier_semaphore()
    peers = [k.dev_z(1), k.dev_z(-1), k.dev_x()] + [k.dev_y(delta) for delta in (1, 2, 3)]
    for peer in peers:
        pl.semaphore_signal(barrier, inc=1, device_id=peer, device_id_type=mesh_id)

    loads = {}

    def start_load(name, src, dst):
        loads[name] = [pltpu.make_async_copy(src, dst, load_sem.at[len(started)])]
        started.append(name)
        loads[name][0].start()

    started = []
    start_load("wk", k.h_wk, k.wkv.at[:, 0:HEAD])
    start_load("wv", k.h_wv, k.wkv.at[:, HEAD : 2 * HEAD])
    for t in range(CHUNKS):
        start_load("tok%d" % t, k.h_tok.at[pl.ds(t * ROWS, ROWS)], k.tok.at[pl.ds(t * ROWS, ROWS)])
    for c in (2, 3, 0, 1):
        cols = slice(c * 512, (c + 1) * 512)
        start_load("wq%d" % c, k.h_wq.at[:, cols], k.wq.at[:, cols])
    start_load("tab", k.h_tab.at[:, k.z * 2 + k.xh], k.tab)
    start_load("wout", k.h_wout, k.wout)

    def load(name):
        if name == "wkv":
            load("wk")
            load("wv")
        elif name in loads:
            loads.pop(name)[0].wait()

    k.load = load
    k.ready = lambda: pl.semaphore_wait(barrier, len(peers))
    sent, waited = {}, set()

    def send(name, src, dst, device):
        i = messages.index(name)
        sent[name] = pltpu.make_async_remote_copy(
            src_ref=src,
            dst_ref=dst,
            send_sem=send_sem.at[i],
            recv_sem=recv_sem.at[i],
            device_id=device,
            device_id_type=mesh_id,
        )
        sent[name].start()

    k.send = send

    def rotate(value, t):
        return value * k.tab[t, :, 0:HEAD] + pltpu.roll(value, HEAD // 2, 1) * k.tab[t, :, HEAD : 2 * HEAD]

    k.rotate = rotate

    def store_query(t, c0, value):
        for i in range(value.shape[1] // HEAD):
            k.qs[t, c0 // HEAD + i] = rotate(value[:, i * HEAD : (i + 1) * HEAD], t).astype(BF)

    k.store_query = store_query

    def mask(t):
        keys = (t + 1) * ROWS
        row = t * ROWS + (k.z * 2 + k.xh) * R + lax.broadcasted_iota(jnp.int32, (R, keys), 0)
        col = lax.broadcasted_iota(jnp.int32, (R, keys), 1)
        docs = jnp.broadcast_to(k.docs[0:1, 0:keys].astype(F32), (R, keys))
        mine = jnp.sum(jnp.where(row == col, docs, 0.0), axis=1, keepdims=True)
        allowed = (docs == mine) & (col <= row)
        k.bias[t, :, 0:keys] = jnp.where(allowed, 0.0, -1e30)

    k.mask = mask

    def attend(t, first, count):
        keys = (t + 1) * ROWS
        query = k.qs[t, first : first + count].reshape(count * R, HEAD)
        key = k.kvf[0 : t + 1, :, :, :, 0:HEAD].reshape(keys, HEAD)
        value = k.kvf[0 : t + 1, :, :, :, HEAD : 2 * HEAD].reshape(keys, HEAD)
        scores = lax.dot_general(query, key, (((1,), (1,)), ((), ())), preferred_element_type=F32)
        scores = (scores * SCALE).reshape(count, R, keys) + k.bias[t, :, 0:keys][None]
        top = jnp.max(scores, axis=-1, keepdims=True)
        weights = jnp.exp2(scores - top)
        total = jnp.sum(weights, axis=-1, keepdims=True)
        mixed = jnp.dot(weights.reshape(count * R, keys).astype(BF), value, preferred_element_type=F32)
        mixed = (mixed.reshape(count, R, HEAD) / total).astype(BF)
        for i in range(count):
            c0 = (first + i) * HEAD
            k.att[t, k.z, k.xh, :, c0 : c0 + HEAD] = mixed[i]

    k.attend = attend

    nodes = {node.name: node for node in build(k)}
    for name in order_names:
        node = nodes[name]
        for message in node.waits:
            if message not in waited:
                waited.add(message)
                sent[message].wait_recv()
        node.emit()
    for name in messages:
        if name not in waited:
            sent[name].wait_recv()
        sent[name].wait_send()
    for name in list(loads):
        load(name)


def shards(tokens, doc_ids, w_query, key_weight, value_weight, w_out):
    nodes = build(None)
    order = [nodes[i] for i in ORDER]
    messages = [send[0] for node in order for send in node.sends]
    scratch = [
        pltpu.VMEM((SEQ, MODEL), BF),
        pltpu.VMEM((MODEL, QCOLS), BF),
        pltpu.VMEM((MODEL, 2 * HEAD), BF),
        pltpu.VMEM((QCOLS, OCOLS), BF),
        pltpu.VMEM((CHUNKS, R, 2 * HEAD), F32),
        pltpu.VMEM((CHUNKS, R, SEQ), F32),
        pltpu.VMEM((CHUNKS, NZ, 2, R, QCOLS), F32),
        pltpu.VMEM((CHUNKS, NZ, 2, R, 2 * HEAD), F32),
        pltpu.VMEM((CHUNKS, NZ, 2, R, 2 * HEAD), BF),
        pltpu.VMEM((CHUNKS, QCOLS // HEAD, R, HEAD), BF),
        pltpu.VMEM((CHUNKS, NZ, 2, R, QCOLS), BF),
        pltpu.VMEM((CHUNKS, NZ, 2 * R, 256), F32),
        pltpu.VMEM((CHUNKS, NY - 1, NZ, 2 * R, 256), BF),
        pltpu.VMEM((CHUNKS, NY - 1, NZ, 2 * R, 256), BF),
    ]
    for shape in buffers().values():
        scratch += [pltpu.VMEM(shape, BF), pltpu.VMEM(shape, BF)]
    scratch += [
        pltpu.SemaphoreType.DMA((len(messages),)),
        pltpu.SemaphoreType.DMA((len(messages),)),
        pltpu.SemaphoreType.DMA((16,)),
    ]
    anywhere = pl.BlockSpec(memory_space=pl.ANY)
    vmem = pl.BlockSpec(memory_space=pltpu.VMEM)
    return pl.pallas_call(
        functools.partial(kernel, [node.name for node in order], messages),
        out_shape=jax.ShapeDtypeStruct((SEQ, 256), BF),
        in_specs=[vmem] + [anywhere] * 6,
        out_specs=vmem,
        scratch_shapes=scratch,
        compiler_params=pltpu.CompilerParams(
            collective_id=0, has_side_effects=True, vmem_limit_bytes=56 * 1024 * 1024
        ),
        name="sublayer",
    )(doc_ids.reshape(1, SEQ), tokens, w_query, key_weight, value_weight, w_out, jnp.asarray(rotary_table()))


def solution(mesh):
    placed = (
        P("dp", "loop"),
        P("dp"),
        P("loop", "column"),
        P("loop", "column"),
        P("loop", "column"),
        P("column", "loop"),
    )
    return jax.shard_map(
        shards, mesh=mesh, in_specs=placed, out_specs=P("dp", ("loop", "column")), check_vma=False
    )
```

time: 503 us -> 100 us (0.20)
  waiting for transfers between devices: 377 us -> 0 us
  Pallas kernels: 0 us -> 98.4 us
  blocking collectives: 76.8 us -> 0 us
  matrix products: 20 us -> 0 us
  between operations: 13.2 us -> 0.01 us
  other arithmetic: 8.78 us -> 0 us
    reduce_scatter x2 -> x0, waiting for transfers between devices: 280 us -> none  [the longest x1 233 us: shards(): lax.psum_scatter(jnp.concatenate([jnp.dot(tokens, w_query, preferred_elem...]
    pallas_call x0 -> x1, Pallas kernels: none -> 98.4 us  [shards(): pl.pallas_call(functools.partial(kernel, [node.name for node in order], m...]
    all_gather x1 -> x0, waiting for transfers between devices: 96.1 us -> none  [shards(): lax.all_gather(attended, 'loop', axis=0, tiled=True)]
    all_gather x2 -> x0, blocking collectives: 76.8 us -> none  [the longest x1 39.9 us: shards(): key_piece = lax.all_gather(key, 'loop', axis=0, tiled=True)]
    dot_general x6 -> x0, matrix products: 20 us -> none  [the longest x1 9.88 us: shards(): jnp.dot(lax.all_gather(attended, 'loop', axis=0, tiled=True), w_out, pref...]
  transfers between devices with their start and end apart: 3 -> 0, of which waited for: 3 -> 0; matrix products, arithmetic and copies ran while one was open for 0% -> 0% of each run, Pallas kernels for 0% -> 0%
where the time goes in v1:
time: 100 us
  Pallas kernels  98.4 us (98%)
  local copies, waits for them, and re-layouts  1.87 us (2%)
    pallas_call x1, Pallas kernels, shards(): pl.pallas_call(functools.partial(kernel, [node.name for node in order], m...  98.4 us

profile of v1, /device:TPU:2, one launch (start us, length us, event | category | flops | bytes accessed | tf_op | source)
XLA Modules:
  0.0 100.3 jit_solution(2234475915248905644)
XLA Ops:
  0.0 98.4 %sublayer.1 = bf16[1024,256]{1,0:T(8,128)(2,1)} custom-call(s32[1,1024]{1,0:T(1,128)} %bitcast.1, bf16[1024,1024]{1,0:T(8,128)(2,1)} %refs_1_.1, bf16[1024,2048]{1,0:T(8,128)(2,1)} %refs_2_.1, bf16[1024,128]{1,0:T(8,128)(2,1)} %refs_3_.1, bf16[1024,128]{1,0:T(8,128)(2,1)} %refs_4_.1, bf16[2048,1024]{1,0:T(8,128)(2,1)} %refs_5_.1, ...), custom_call_target="tpu_custom_call" | custom-call | tf_op jit(solution)/shard_map/sublayer/pallas_call | solution.py:595
  98.5 1.9 %copy.9 = bf16[1024,256]{1,0:T(8,128)(2,1)} copy(bf16[1024,256]{1,0:T(8,128)(2,1)} %sublayer.1) | data formatting | bytes 1048576

commit v2 on v1

--- a/solution.py
+++ b/solution.py
@@ -19,23 +19,24 @@
 CHUNKS = 2
 ROWS = SEQ // CHUNKS
 R = ROWS // (2 * NZ)
-XFIRST = ((0, 640), (640, 640))
-ZFIRST = ((1280, 384), (1664, 384))
+XFIRST = ((0, 768), (768, 640))
+ZFIRST = ((1408, 640),)
+QUERY_PARTS = (2, 3, 0, 1)
+XWIDTH = sum(width for _, width in XFIRST)
+OUTS = (((0,), (1,), (2,), (3,), (4,)), ((0,), (1,), (2,), (3,), (4,)))
 BF = jnp.bfloat16
 F32 = jnp.float32
 SCALE = math.log2(math.e) / math.sqrt(HEAD)
 ORDER = (
-    0, 13, 21, 9, 5, 18, 1, 148, 45, 152, 4, 82, 79, 14, 75, 10, 3, 19, 22, 60, 46, 149, 76, 81, 2, 53, 59, 153,
-    80, 11, 78, 64, 6, 157, 41, 7, 160, 77, 63, 61, 23, 15, 65, 83, 12, 150, 54, 50, 42, 24, 86, 16, 62, 158, 161,
-    91, 66, 67, 55, 8, 47, 20, 43, 182, 17, 87, 189, 151, 71, 183, 68, 187, 56, 27, 30, 159, 162, 25, 51, 154, 167,
-    188, 184, 166, 84, 44, 31, 26, 69, 88, 28, 72, 186, 185, 193, 32, 85, 169, 34, 170, 163, 173, 171, 70, 38, 155,
-    168, 48, 190, 73, 33, 29, 172, 52, 177, 194, 89, 174, 35, 39, 74, 191, 94, 178, 57, 175, 195, 36, 90, 114, 95,
-    127, 110, 49, 124, 92, 198, 179, 58, 196, 192, 40, 37, 164, 93, 111, 115, 125, 128, 134, 180, 100, 117, 96,
-    121, 165, 106, 176, 156, 200, 103, 116, 131, 197, 202, 199, 122, 231, 234, 129, 112, 181, 201, 97, 220, 101,
-    135, 217, 232, 104, 107, 210, 126, 113, 118, 132, 140, 203, 238, 235, 221, 123, 245, 218, 241, 207, 102, 227,
-    119, 233, 224, 213, 142, 108, 222, 130, 136, 236, 138, 246, 208, 105, 228, 98, 133, 219, 214, 239, 247, 242,
-    240, 204, 211, 223, 225, 137, 109, 99, 144, 141, 237, 120, 215, 209, 205, 243, 226, 212, 143, 229, 249, 146,
-    230, 248, 216, 206, 244, 251, 253, 250, 147, 145, 252, 139, 254,
+    0, 11, 7, 3, 64, 16, 70, 19, 1, 39, 67, 43, 12, 8, 69, 68, 66, 65, 17, 2, 53, 4, 20, 40, 133, 54, 9, 71, 21,
+    49, 48, 13, 129, 51, 80, 44, 10, 72, 18, 75, 41, 22, 5, 14, 50, 170, 139, 52, 55, 60, 56, 134, 6, 155, 45, 23,
+    42, 130, 15, 144, 28, 158, 138, 61, 154, 25, 57, 73, 143, 76, 29, 62, 46, 157, 141, 156, 161, 24, 160, 159, 26,
+    58, 165, 32, 36, 131, 140, 74, 142, 145, 30, 77, 135, 37, 59, 27, 149, 47, 33, 146, 166, 31, 132, 78, 63, 162,
+    34, 150, 82, 95, 91, 79, 167, 163, 136, 151, 147, 83, 38, 81, 35, 164, 168, 96, 102, 152, 108, 148, 105, 92,
+    137, 98, 171, 169, 173, 198, 84, 153, 172, 184, 106, 181, 109, 112, 97, 115, 195, 103, 119, 199, 93, 185, 174,
+    191, 107, 88, 110, 104, 182, 99, 178, 209, 113, 200, 205, 186, 120, 188, 196, 85, 89, 175, 202, 111, 94, 117,
+    116, 179, 114, 206, 100, 192, 201, 183, 187, 197, 203, 121, 86, 90, 176, 189, 207, 211, 180, 193, 204, 190,
+    123, 194, 101, 208, 118, 87, 125, 177, 213, 215, 217, 127, 212, 126, 122, 214, 210, 218, 124, 216, 128,
 )
 
 
@@ -71,7 +72,7 @@
     angles = np.arange(SEQ, dtype=np.float64)[:, None] * frequency
     cosine, sine = np.cos(angles), np.sin(angles)
     table = np.concatenate([cosine, cosine, -sine, sine], 1).astype(np.float32)
-    return table.reshape(CHUNKS, 2 * NZ, R, 2 * HEAD)
+    return table.reshape(CHUNKS, NZ, 2, R, 2 * HEAD)
 
 
 def split(parity):
@@ -93,23 +94,26 @@
             k.load("tok%d" % t)
             res = jnp.dot(k.tok[pl.ds(t * ROWS, ROWS)], k.wkv[...], preferred_element_type=F32)
             k.pkv[t] = res.reshape(NZ, 2, R, 2 * HEAD)
+        k.query_loads()
         k.ready()
 
-    add("kvmm", 0, 3.0, [], [], [], emit_kv)
+    add("kvmm", 0, 4.0, [], [], [], emit_kv)
 
     def emit_q(t, c0, width):
-        k.load("tok%d" % t)
         for c in range(c0 // 512, (c0 + width - 1) // 512 + 1):
             k.load("wq%d" % c)
         res = jnp.dot(k.tok[pl.ds(t * ROWS, ROWS)], k.wq[:, c0 : c0 + width], preferred_element_type=F32)
         k.pq[t, :, :, :, c0 : c0 + width] = res.reshape(NZ, 2, R, width)
+        if k.last_loads:
+            k.last_loads()
+            k.last_loads = None
 
     for t in range(CHUNKS):
         for c0, width in ZFIRST + XFIRST:
             add(
                 "q%d_%d" % (t, c0),
                 1 + t * 40 + (0.1 if c0 < ZFIRST[0][0] else 0),
-                width / 600.0,
+                width / 620.0,
                 ["kvmm"],
                 [],
                 [],
@@ -128,7 +132,7 @@
                     if s > 0:
                         value = value + up(k.buf[tag, "r"][base + s - 1])
                     k.buf[tag, "s"][base + s] = down(value)
-                    k.send(name, k.buf[tag, "s"].at[base + s], k.buf[tag, "r"].at[base + s], k.dev_z(sign))
+                    k.send(name, k.buf[tag, "s"].at[base + s], k.buf[tag, "r"].at[base + s], k.dev_z(sign), tag, k.buf[tag, "s"])
 
                 waits = list(step_waits(sign, s))
                 after = list(start_after)
@@ -148,7 +152,7 @@
             tag,
             base + 2,
             4,
-            0.15,
+            0.2,
             2 * R * 768,
             counts,
             lambda sign, s, d, t=t: k.pkv[t, d],
@@ -158,37 +162,36 @@
             widen_pair,
         )
 
+        def kv_pair(t, tag, counts):
+            return k.pkv[t, k.z] + ring_sum(tag, counts, lambda b, i: b[i], widen_pair)
+
         def emit_kv_fin(t=t, tag=tag, counts=counts):
-            o = 1 - k.xh
-            value = k.pkv[t, k.z, o] + ring_sum(tag, counts, lambda b, i: b[i, o], widen_pair)
-            k.buf[tag + "x", "s"][...] = narrow_pair(value)
+            k.buf[tag + "x", "s"][...] = narrow_pair(kv_pair(t, tag, counts))
             k.send(tag + "x", k.buf[tag + "x", "s"], k.buf[tag + "x", "r"], k.dev_x())
 
-        add(tag + "fin", base + 2, 0.12, last, last, [(tag + "x", ["x"], R * 768)], emit_kv_fin)
+        add(tag + "fin", base + 2, 0.2, last, last, [(tag + "x", ["x"], 2 * R * 768)], emit_kv_fin)
 
         def emit_kv_own(t=t, tag=tag, counts=counts):
             k.load("tab")
-            value = k.pkv[t, k.z, k.xh] + ring_sum(tag, counts, lambda b, i: b[i, k.xh], widen_pair)
-            value = value + widen_pair(k.buf[tag + "x", "r"][...])
-            k.kvf[t, k.z, k.xh, :, 0:HEAD] = k.rotate(value[:, 0:HEAD], t).astype(BF)
-            k.kvf[t, k.z, k.xh, :, HEAD : 2 * HEAD] = value[:, HEAD : 2 * HEAD].astype(BF)
-            here = k.kvf.at[t, k.z, k.xh]
-            k.send("kgx%d" % t, here, here, k.dev_x())
-
-        add(tag + "own", base + 2, 0.2, [tag + "fin"], [tag + "x"], [("kgx%d" % t, ["x"], R * 512)], emit_kv_own)
-
-    def gather(tag, rank, stride, size, counts, block, start_after, start_waits):
+            value = kv_pair(t, tag, counts) + widen_pair(k.buf[tag + "x", "r"][...])
+            for i in range(2):
+                k.kvf[t, k.z, i, :, 0:HEAD] = k.rotate(value[i, :, 0:HEAD], t, i).astype(BF)
+            k.kvf[t, k.z, :, :, HEAD : 2 * HEAD] = value[:, :, HEAD : 2 * HEAD].astype(BF)
+
+        add(tag + "own", base + 2, 0.3, [tag + "fin"], [tag + "x"], [], emit_kv_own)
+
+    def gather(tag, rank, stride, size, counts, block, start_after, start_waits, seven):
         for sign, n in ((1, counts[0]), (-1, counts[1])):
             for s in range(n):
                 name = (tag, sign, s)
 
                 def emit(sign=sign, s=s, name=name):
                     here = block(k.zi(-sign * s))
-                    k.send(name, here, here, k.dev_z(sign))
+                    k.send(name, here, here, k.dev_z(sign), tag, seven())
 
                 after = list(start_after) if s == 0 else [(tag, sign, s - 1)]
                 waits = list(start_waits) if s == 0 else [(tag, sign, s - 1)]
-                add(name, rank + stride * s, 0.05, after, waits, [(name, zlink(sign), size)], emit)
+                add(name, rank + stride * s, 0.1, after, waits, [(name, zlink(sign), size)], emit)
         return [(tag, 1, counts[0] - 1), (tag, -1, counts[1] - 1)]
 
     kg_last = [
@@ -200,7 +203,8 @@
             split(1 - t),
             lambda d, t=t: k.kvf.at[t, d],
             ["kv%down" % t],
-            ["kgx%d" % t],
+            [],
+            lambda t=t: k.kvf.at[t, 0 : NZ - 1],
         )
         for t in range(CHUNKS)
     ]
@@ -214,7 +218,7 @@
                 tag,
                 base + 3 + 0.2 * j,
                 8,
-                0.15,
+                0.2,
                 2 * R * width * 2,
                 counts,
                 lambda sign, s, d, c0=c0, width=width, t=t: k.pq[t, d, :, :, c0 : c0 + width],
@@ -228,14 +232,14 @@
                 k.buf[tag + "x", "s"][...] = value.astype(BF)
                 k.send(tag + "x", k.buf[tag + "x", "s"], k.buf[tag + "x", "r"], k.dev_x())
 
-            add(tag + "fin", base + 36, 0.1, last, last, [(tag + "x", ["x"], R * width * 2)], emit_fin)
+            add(tag + "fin", base + 36, 0.2, last, last, [(tag + "x", ["x"], R * width * 2)], emit_fin)
 
             def emit_own(t=t, tag=tag, c0=c0, width=width, counts=counts):
                 k.load("tab")
                 value = k.pq[t, k.z, k.xh, :, c0 : c0 + width] + ring_sum(tag, counts, lambda b, i: b[i, k.xh])
                 k.store_query(t, c0, value + k.buf[tag + "x", "r"][...].astype(F32))
 
-            add(tag + "own", base + 37, 0.15, [tag + "fin"], [tag + "x"], [], emit_own)
+            add(tag + "own", base + 37, 0.25, [tag + "fin"], [tag + "x"], [], emit_own)
             own_nodes[c0] = tag + "own"
 
         for j, (c0, width) in enumerate(XFIRST):
@@ -252,12 +256,19 @@
 
                 def emit_x(t=t, tag=tag, i=i, c0=c0, width=width, where=where):
                     k.buf[tag + "x", "s"][i] = k.pq[t, where(i), 1 - k.xh, :, c0 : c0 + width].astype(BF)
-                    k.send((tag, "x", i), k.buf[tag + "x", "s"].at[i], k.buf[tag + "x", "r"].at[i], k.dev_x())
+                    k.send(
+                        (tag, "x", i),
+                        k.buf[tag + "x", "s"].at[i],
+                        k.buf[tag + "x", "r"].at[i],
+                        k.dev_x(),
+                        tag + "x",
+                        k.buf[tag + "x", "s"],
+                    )
 
                 add(
                     (tag, "x", i),
                     base + 4 + 0.1 * place - (8 if t else 0),
-                    0.06,
+                    0.1,
                     ["q%d_%d" % (t, c0)],
                     [],
                     [((tag, "x", i), ["x"], R * width * 2)],
@@ -272,7 +283,7 @@
                 tag,
                 base + 9,
                 8,
-                0.15,
+                0.2,
                 R * width * 2,
                 counts,
                 own_xf,
@@ -285,11 +296,11 @@
                 value = k.pq[t, k.z, k.xh, :, c0 : c0 + width] + k.buf[tag + "x", "r"][NZ - 1].astype(F32)
                 k.store_query(t, c0, value + ring_sum(tag, counts, lambda b, i: b[i]))
 
-            add(tag + "own", base + 37.5, 0.15, last, last + [(tag, "x", NZ - 1)], [], emit_xf_own)
+            add(tag + "own", base + 37.5, 0.25, last, last + [(tag, "x", NZ - 1)], [], emit_xf_own)
             own_nodes[c0] = tag + "own"
 
         add("mask%d" % t, base + 20, 0.3, ["kvmm"], [], [], functools.partial(lambda t: k.mask(t), t))
-        keys_in = [m for u in range(t + 1) for m in ["kgx%d" % u] + kg_last[u]]
+        keys_in = [m for u in range(t + 1) for m in kg_last[u]]
         keys_after = [m for u in range(t + 1) for m in ["kv%down" % u] + kg_last[u]]
         for place, (c0, width) in enumerate(ZFIRST + XFIRST):
             gtag = "g%d_%d" % (t, c0)
@@ -297,12 +308,15 @@
             def emit_att(t=t, gtag=gtag, c0=c0, width=width):
                 k.attend(t, c0 // HEAD, width // HEAD)
                 here = k.att.at[t, k.z, k.xh, :, c0 : c0 + width]
-                k.send((gtag, "x", 0), here, here, k.dev_x())
+                count = NZ if (c0, width) in XFIRST else 1
+                k.send(
+                    (gtag, "x", 0), here, here, k.dev_x(), gtag + "x", k.att.at[t, 0:count, 0, :, c0 : c0 + width]
+                )
 
             add(
                 gtag + "att",
                 base + 40 + place,
-                width / 1000.0 + 0.05,
+                width / 1700.0 + 0.15,
                 [own_nodes[c0], "mask%d" % t] + keys_after,
                 keys_in,
                 [((gtag, "x", 0), ["x"], R * width * 2)],
@@ -320,6 +334,7 @@
                 lambda d, t=t, c0=c0, width=width: k.att.at[t, d, :, :, c0 : c0 + width],
                 [gtag + "att"],
                 [(gtag, "x", 0)],
+                lambda t=t, c0=c0, width=width: k.att.at[t, 0 : NZ - 1, :, :, c0 : c0 + width],
             )
             last_step.append((gtag, False, split(j)))
         for j, (c0, width) in enumerate(XFIRST):
@@ -333,41 +348,54 @@
                 lambda d, t=t, c0=c0, width=width: k.att.at[t, d, k.xh, :, c0 : c0 + width],
                 [gtag + "att"],
                 [],
+                lambda t=t, c0=c0, width=width: k.att.at[t, 0 : NZ - 1, 0, :, c0 : c0 + width],
             )
             last_step.append((gtag, True, counts))
             for sign, n in ((1, counts[0]), (-1, counts[1])):
                 for s in range(n):
                     name = (gtag, "x", sign, s)
 
-                    def emit_pass(t=t, sign=sign, s=s, name=name, c0=c0, width=width):
+                    def emit_pass(t=t, gtag=gtag, sign=sign, s=s, name=name, c0=c0, width=width):
                         here = k.att.at[t, k.zi(-sign * (s + 1)), k.xh, :, c0 : c0 + width]
-                        k.send(name, here, here, k.dev_x())
+                        blocks = 1 if s == 3 else 2
+                        k.send(
+                            name,
+                            here,
+                            here,
+                            k.dev_x(),
+                            gtag + "x",
+                            k.att.at[t, 0:NZ, 0, :, c0 : c0 + width],
+                            ("pass", t, s),
+                            k.att.at[t, 0:blocks, 0, :, 0:XWIDTH],
+                        )
 
                     after = [(gtag, sign, s + 1)] if s + 1 < n else [(gtag, sign, s)]
                     add(
                         name,
                         base + 43.5 + 4 * s,
-                        0.05,
+                        0.1,
                         after,
                         [(gtag, sign, s)],
                         [(name, ["x"], R * width * 2)],
                         emit_pass,
                     )
-        for r in range(5):
-            shifts = [0] if r == 0 else [4] if r == 4 else [-r, r]
-            first = 0 if r == 0 else 2 * r - 1
+        for rounds in OUTS[t]:
+            r = rounds[-1]
+            shifts, first = [], (2 * rounds[0] - 1 if rounds[0] else 0)
             waits, after = [], []
-            for gtag, passes, counts in last_step:
-                if r == 0:
-                    waits.append((gtag, "x", 0))
-                    after.append(gtag + "att")
-                for sign, n in ((1, counts[0]), (-1, counts[1])):
-                    if 0 < r <= n:
-                        waits.append((gtag, sign, r - 1))
-                        after.append((gtag, sign, r - 1))
-                        if passes:
-                            waits.append((gtag, "x", sign, r - 1))
-                            after.append((gtag, "x", sign, r - 1))
+            for q in rounds:
+                shifts += [0] if q == 0 else [4] if q == 4 else [-q, q]
+                for gtag, passes, counts in last_step:
+                    if q == 0:
+                        waits.append((gtag, "x", 0))
+                        after.append(gtag + "att")
+                    for sign, n in ((1, counts[0]), (-1, counts[1])):
+                        if 0 < q <= n:
+                            waits.append((gtag, sign, q - 1))
+                            after.append((gtag, sign, q - 1))
+                            if passes:
+                                waits.append((gtag, "x", sign, q - 1))
+                                after.append((gtag, "x", sign, q - 1))
 
             def emit_out(t=t, r=r, shifts=shifts, first=first):
                 k.load("wout")
@@ -387,13 +415,17 @@
                             k.ys.at[t, delta - 1, first : first + count],
                             k.yr.at[t, delta - 1, first : first + count],
                             k.dev_y(delta),
+                            "y",
+                            k.ys,
+                            ("y", t, r),
+                            k.yr.at[t, :, first : first + count],
                         )
 
             size = len(shifts) * 2 * R * 512
             add(
                 ("out", t, r),
                 base + 45 + 4 * r,
-                1.4,
+                0.55 + 0.15 + 0.0024 * 2 * R * len(shifts),
                 after,
                 waits,
                 [(("y", t, r, 2), ["y+", "y-"], size), (("y", t, r, 1), ["y+"], size), (("y", t, r, 3), ["y-"], size)],
@@ -406,12 +438,12 @@
                     for delta in range(NY - 1):
                         total = total + k.yr[t, delta, first + i].astype(F32)
                     row = pl.multiple_of(t * ROWS + k.zi(shift) * 2 * R, 2 * R)
-                    k.out[pl.ds(row, 2 * R), :] = total.astype(BF)
+                    k.out[pl.ds(row, 2 * R), :] = total
 
             add(
                 ("fin", t, r),
                 base + 50 + 4 * r,
-                0.15,
+                0.15 + 0.05 * len(shifts),
                 [("out", t, r)],
                 [("y", t, r, delta) for delta in (1, 2, 3)],
                 [],
@@ -424,7 +456,7 @@
     shapes = {}
     for t in range(CHUNKS):
         shapes["kv%d" % t] = (7, 2, R, 384)
-        shapes["kv%dx" % t] = (R, 384)
+        shapes["kv%dx" % t] = (2, R, 384)
         for c0, width in ZFIRST:
             shapes["zf%d_%d" % (t, c0)] = (7, 2, R, width)
             shapes["zf%d_%dx" % (t, c0)] = (R, width)
@@ -464,57 +496,84 @@
     for peer in peers:
         pl.semaphore_signal(barrier, inc=1, device_id=peer, device_id_type=mesh_id)
 
-    loads = {}
+    loads, started = {}, []
 
     def start_load(name, src, dst):
-        loads[name] = [pltpu.make_async_copy(src, dst, load_sem.at[len(started)])]
+        loads[name] = pltpu.make_async_copy(src, dst, load_sem.at[len(started)])
         started.append(name)
-        loads[name][0].start()
-
-    started = []
-    start_load("wk", k.h_wk, k.wkv.at[:, 0:HEAD])
-    start_load("wv", k.h_wv, k.wkv.at[:, HEAD : 2 * HEAD])
-    for t in range(CHUNKS):
-        start_load("tok%d" % t, k.h_tok.at[pl.ds(t * ROWS, ROWS)], k.tok.at[pl.ds(t * ROWS, ROWS)])
-    for c in (2, 3, 0, 1):
-        cols = slice(c * 512, (c + 1) * 512)
-        start_load("wq%d" % c, k.h_wq.at[:, cols], k.wq.at[:, cols])
-    start_load("tab", k.h_tab.at[:, k.z * 2 + k.xh], k.tab)
-    start_load("wout", k.h_wout, k.wout)
+        loads[name].start()
+
+    def first_loads():
+        start_load("wk", k.h_wk, k.wkv.at[:, 0:HEAD])
+        start_load("wv", k.h_wv, k.wkv.at[:, HEAD : 2 * HEAD])
+        for t in range(CHUNKS):
+            start_load("tok%d" % t, k.h_tok.at[pl.ds(t * ROWS, ROWS)], k.tok.at[pl.ds(t * ROWS, ROWS)])
+
+    def query_loads():
+        for c in QUERY_PARTS:
+            cols = slice(c * 512, (c + 1) * 512)
+            start_load("wq%d" % c, k.h_wq.at[:, cols], k.wq.at[:, cols])
+
+    def last_loads():
+        start_load("tab", k.h_tab.at[:, k.z], k.tab)
+        start_load("wout", k.h_wout, k.wout)
+
+    first_loads()
+    k.query_loads, k.last_loads = query_loads, last_loads
 
     def load(name):
+        if name in ("tab", "wout") and k.last_loads:
+            k.last_loads()
+            k.last_loads = None
         if name == "wkv":
             load("wk")
             load("wv")
         elif name in loads:
-            loads.pop(name)[0].wait()
+            loads.pop(name).wait()
 
     k.load = load
     k.ready = lambda: pl.semaphore_wait(barrier, len(peers))
-    sent, waited = {}, set()
-
-    def send(name, src, dst, device):
-        i = messages.index(name)
+    sent, waited, send_groups, recv_groups, recv_wholes = {}, set(), {}, {}, {}
+
+    def send(name, src, dst, device, group=None, whole=None, recv=None, recv_whole=None):
+        group, recv = group or name, recv or name
+        i = list(send_groups).index(group) if group in send_groups else len(send_groups)
+        j = recv_ids.setdefault(recv, len(recv_ids))
         sent[name] = pltpu.make_async_remote_copy(
             src_ref=src,
             dst_ref=dst,
             send_sem=send_sem.at[i],
-            recv_sem=recv_sem.at[i],
+            recv_sem=recv_sem.at[j],
             device_id=device,
             device_id_type=mesh_id,
         )
         sent[name].start()
-
+        recv_groups[name] = recv
+        if group not in send_groups:
+            ref = src if whole is None else whole
+            send_groups[group] = pltpu.make_async_remote_copy(ref, ref, send_sem.at[i], recv_sem.at[j], device, mesh_id)
+        if recv not in recv_wholes:
+            ref = dst if recv_whole is None else recv_whole
+            recv_wholes[recv] = pltpu.make_async_remote_copy(ref, ref, send_sem.at[i], recv_sem.at[j], device, mesh_id)
+
+    def receive(name):
+        recv = recv_groups[name]
+        if recv not in waited:
+            waited.add(recv)
+            recv_wholes[recv].wait_recv()
+
+    recv_ids = {}
     k.send = send
 
-    def rotate(value, t):
-        return value * k.tab[t, :, 0:HEAD] + pltpu.roll(value, HEAD // 2, 1) * k.tab[t, :, HEAD : 2 * HEAD]
+    def rotate(value, t, half):
+        table = k.tab[t, half]
+        return value * table[:, 0:HEAD] + pltpu.roll(value, HEAD // 2, 1) * table[:, HEAD : 2 * HEAD]
 
     k.rotate = rotate
 
     def store_query(t, c0, value):
         for i in range(value.shape[1] // HEAD):
-            k.qs[t, c0 // HEAD + i] = rotate(value[:, i * HEAD : (i + 1) * HEAD], t).astype(BF)
+            k.qs[t, c0 // HEAD + i] = rotate(value[:, i * HEAD : (i + 1) * HEAD], t, k.xh).astype(BF)
 
     k.store_query = store_query
 
@@ -551,28 +610,46 @@
     for name in order_names:
         node = nodes[name]
         for message in node.waits:
-            if message not in waited:
-                waited.add(message)
-                sent[message].wait_recv()
+            receive(message)
         node.emit()
     for name in messages:
-        if name not in waited:
-            sent[name].wait_recv()
-        sent[name].wait_send()
+        receive(name)
+    for copy in send_groups.values():
+        copy.wait_send()
     for name in list(loads):
         load(name)
+
+
+def semaphores(messages):
+    sends, receives = set(), set()
+    for name in messages:
+        group, receive = name, name
+        if isinstance(name, tuple):
+            tag = name[0]
+            if tag == "y":
+                group, receive = "y", name[:3]
+            elif name[1] == "x":
+                group = tag + "x"
+                if len(name) == 4:
+                    receive = ("pass", tag[:2], name[3])
+            else:
+                group = tag
+        sends.add(group)
+        receives.add(receive)
+    return len(sends), len(receives)
 
 
 def shards(tokens, doc_ids, w_query, key_weight, value_weight, w_out):
     nodes = build(None)
     order = [nodes[i] for i in ORDER]
     messages = [send[0] for node in order for send in node.sends]
+    sends, receives = semaphores(messages)
     scratch = [
         pltpu.VMEM((SEQ, MODEL), BF),
         pltpu.VMEM((MODEL, QCOLS), BF),
         pltpu.VMEM((MODEL, 2 * HEAD), BF),
         pltpu.VMEM((QCOLS, OCOLS), BF),
-        pltpu.VMEM((CHUNKS, R, 2 * HEAD), F32),
+        pltpu.VMEM((CHUNKS, 2, R, 2 * HEAD), F32),
         pltpu.VMEM((CHUNKS, R, SEQ), F32),
         pltpu.VMEM((CHUNKS, NZ, 2, R, QCOLS), F32),
         pltpu.VMEM((CHUNKS, NZ, 2, R, 2 * HEAD), F32),
@@ -586,15 +663,15 @@
     for shape in buffers().values():
         scratch += [pltpu.VMEM(shape, BF), pltpu.VMEM(shape, BF)]
     scratch += [
-        pltpu.SemaphoreType.DMA((len(messages),)),
-        pltpu.SemaphoreType.DMA((len(messages),)),
+        pltpu.SemaphoreType.DMA((sends,)),
+        pltpu.SemaphoreType.DMA((receives,)),
         pltpu.SemaphoreType.DMA((16,)),
     ]
     anywhere = pl.BlockSpec(memory_space=pl.ANY)
     vmem = pl.BlockSpec(memory_space=pltpu.VMEM)
     return pl.pallas_call(
         functools.partial(kernel, [node.name for node in order], messages),
-        out_shape=jax.ShapeDtypeStruct((SEQ, 256), BF),
+        out_shape=jax.ShapeDtypeStruct((SEQ, 256), F32),
         in_specs=[vmem] + [anywhere] * 6,
         out_specs=vmem,
         scratch_shapes=scratch,
@@ -602,7 +679,7 @@
             collective_id=0, has_side_effects=True, vmem_limit_bytes=56 * 1024 * 1024
         ),
         name="sublayer",
-    )(doc_ids.reshape(1, SEQ), tokens, w_query, key_weight, value_weight, w_out, jnp.asarray(rotary_table()))
+    )(doc_ids.reshape(1, SEQ), tokens, w_query, key_weight, value_weight, w_out, jnp.asarray(rotary_table())).astype(BF)
 
 
 def solution(mesh):

time: 100 us -> 97.1 us (0.971)
  Pallas kernels: 98.4 us -> 94.7 us
  other arithmetic: 0 us -> 2.07 us
  local copies, waits for them, and re-layouts: 1.87 us -> 0 us
    pallas_call x1, Pallas kernels: 98.4 us -> 94.7 us  [shards(): pl.pallas_call(functools.partial(kernel, [node.name for node in order], m...]
    convert_element_type x0 -> x1, other arithmetic: none -> 2.07 us  [shards(): return pl.pallas_call(functools.partial(kernel, [node.name for node in or...]
    unnamed x1 -> x0, local copies, waits for them, and re-layouts: 1.87 us -> none
where the time goes in v2:
time: 97.1 us; the launch traced here: 96.8 us
  Pallas kernels  94.7 us (98%)
  other arithmetic  2.07 us (2%)
    pallas_call x1, Pallas kernels, shards(): pl.pallas_call(functools.partial(kernel, [node.name for node in order], m...  94.7 us
    convert_element_type x1, other arithmetic, shards(): return pl.pallas_call(functools.partial(kernel, [node.name for node in or...  2.07 us

profile of v2, /device:TPU:2, one launch (start us, length us, event | category | flops | bytes accessed | tf_op | source)
XLA Modules:
  0.0 96.8 jit_solution(10084194331740248451)
XLA Ops:
  0.0 94.7 %sublayer.1 = f32[1024,256]{1,0:T(8,128)} custom-call(s32[1,1024]{1,0:T(1,128)} %bitcast.1, bf16[1024,1024]{1,0:T(8,128)(2,1)} %refs_1_.1, bf16[1024,2048]{1,0:T(8,128)(2,1)} %refs_2_.1, bf16[1024,128]{1,0:T(8,128)(2,1)} %refs_3_.1, bf16[1024,128]{1,0:T(8,128)(2,1)} %refs_4_.1, bf16[2048,1024]{1,0:T(8,128)(2,1)} %refs_5_.1, ...), custom_call_target="tpu_custom_call" | custom-call | tf_op jit(solution)/shard_map/sublayer/pallas_call | solution.py:672
  94.7 2.1 %convert_element_type.3 = bf16[1024,256]{1,0:T(8,128)(2,1)} convert(f32[1024,256]{1,0:T(8,128)} %sublayer.1) | non-fusion elementwise | flops 262144 | bytes 1572864 | tf_op jit(solution)/shard_map/convert_element_type | solution.py:682

commit v3 on v2

--- a/solution.py
+++ b/solution.py
@@ -19,24 +19,26 @@
 CHUNKS = 2
 ROWS = SEQ // CHUNKS
 R = ROWS // (2 * NZ)
-XFIRST = ((0, 768), (768, 640))
-ZFIRST = ((1408, 640),)
+XFIRST = ((0, 1024),)
+ZFIRST = ((1024, 512), (1536, 512))
 QUERY_PARTS = (2, 3, 0, 1)
-XWIDTH = sum(width for _, width in XFIRST)
+QUARTER = QCOLS // 4
+PIECES = 4
+PIECE = QUARTER // PIECES
 OUTS = (((0,), (1,), (2,), (3,), (4,)), ((0,), (1,), (2,), (3,), (4,)))
 BF = jnp.bfloat16
 F32 = jnp.float32
 SCALE = math.log2(math.e) / math.sqrt(HEAD)
 ORDER = (
-    0, 11, 7, 3, 64, 16, 70, 19, 1, 39, 67, 43, 12, 8, 69, 68, 66, 65, 17, 2, 53, 4, 20, 40, 133, 54, 9, 71, 21,
-    49, 48, 13, 129, 51, 80, 44, 10, 72, 18, 75, 41, 22, 5, 14, 50, 170, 139, 52, 55, 60, 56, 134, 6, 155, 45, 23,
-    42, 130, 15, 144, 28, 158, 138, 61, 154, 25, 57, 73, 143, 76, 29, 62, 46, 157, 141, 156, 161, 24, 160, 159, 26,
-    58, 165, 32, 36, 131, 140, 74, 142, 145, 30, 77, 135, 37, 59, 27, 149, 47, 33, 146, 166, 31, 132, 78, 63, 162,
-    34, 150, 82, 95, 91, 79, 167, 163, 136, 151, 147, 83, 38, 81, 35, 164, 168, 96, 102, 152, 108, 148, 105, 92,
-    137, 98, 171, 169, 173, 198, 84, 153, 172, 184, 106, 181, 109, 112, 97, 115, 195, 103, 119, 199, 93, 185, 174,
-    191, 107, 88, 110, 104, 182, 99, 178, 209, 113, 200, 205, 186, 120, 188, 196, 85, 89, 175, 202, 111, 94, 117,
-    116, 179, 114, 206, 100, 192, 201, 183, 187, 197, 203, 121, 86, 90, 176, 189, 207, 211, 180, 193, 204, 190,
-    123, 194, 101, 208, 118, 87, 125, 177, 213, 215, 217, 127, 212, 126, 122, 214, 210, 218, 124, 216, 128,
+    0, 8, 206, 7, 4, 9, 15, 14, 2, 203, 1, 117, 11, 10, 29, 3, 48, 18, 17, 16, 47, 5, 125, 6, 138, 38, 12, 113, 30,
+    51, 41, 197, 49, 122, 118, 33, 42, 13, 126, 31, 63, 133, 23, 50, 132, 54, 39, 19, 134, 52, 53, 114, 131, 123,
+    43, 200, 136, 59, 115, 32, 55, 21, 135, 137, 24, 34, 60, 20, 25, 142, 22, 56, 35, 147, 44, 127, 143, 139, 40,
+    128, 36, 119, 27, 116, 124, 57, 45, 140, 144, 201, 120, 61, 129, 58, 28, 26, 141, 37, 145, 64, 71, 46, 65, 77,
+    67, 74, 207, 198, 121, 62, 66, 202, 130, 84, 81, 149, 161, 158, 148, 154, 204, 146, 150, 88, 168, 165, 172,
+    151, 208, 68, 82, 72, 78, 93, 199, 205, 85, 159, 155, 169, 75, 162, 173, 166, 177, 79, 152, 90, 174, 95, 69,
+    86, 76, 83, 179, 100, 163, 156, 153, 167, 184, 91, 170, 182, 70, 175, 80, 73, 180, 160, 87, 98, 164, 89, 96,
+    157, 171, 185, 101, 105, 178, 110, 189, 94, 194, 192, 187, 103, 111, 106, 108, 190, 195, 183, 99, 193, 186, 92,
+    112, 188, 104, 107, 97, 176, 181, 102, 109, 191, 196,
 )
 
 
@@ -147,33 +149,110 @@
         return up(pick(bufs, counts[0] - 1)) + up(pick(bufs, NZ - 2))
 
     for t in range(CHUNKS):
-        tag, counts, base = "kv%d" % t, split(t), 20 * t
-        last = ring(
-            tag,
+        tag, base = "kv%d" % t, 20 * t
+        unit = 2 * R * 512
+
+        def emit_far(sign, t=t, tag=tag):
+            half, slot = (0, 0) if sign > 0 else (1, 1)
+            buf, quarter_buf = k.buf[tag, "s"], k.buf[tag + "q", "s"]
+            buf[slot] = k.pkv[t, k.zi(3 * sign)].astype(BF)
+            k.send((tag, "m", slot), buf.at[slot], k.buf[tag, "r"].at[slot], k.dev_z(sign), tag, buf)
+            cols = slice(half * HEAD, (half + 1) * HEAD)
+            quarter_buf[half] = k.pkv[t, k.zi(4), :, :, cols].astype(BF)
+            k.send(
+                (tag, "q", half),
+                quarter_buf.at[half],
+                k.buf[tag + "q", "r"].at[half],
+                k.dev_z(2 * sign),
+                tag + "q",
+                quarter_buf,
+            )
+
+        def emit_near(t=t, tag=tag):
+            for sign in (1, -1):
+                slot = 2 if sign > 0 else 3
+                k.buf[tag, "s"][slot] = k.pkv[t, k.zi(sign)].astype(BF)
+                k.send(
+                    (tag, "m", slot),
+                    k.buf[tag, "s"].at[slot],
+                    k.buf[tag, "r"].at[slot],
+                    k.dev_z(sign),
+                    tag,
+                    k.buf[tag, "s"],
+                )
+
+        def emit_on(sign, t=t, tag=tag):
+            half, slot = (0, 4) if sign > 0 else (1, 5)
+            value = k.pkv[t, k.zi(2 * sign)] + k.buf[tag, "r"][slot - 4].astype(F32)
+            extra = k.buf[tag + "q", "r"][half].astype(F32)
+            parts = [value[..., 0:HEAD], value[..., HEAD : 2 * HEAD]]
+            parts[half] = parts[half] + extra
+            k.buf[tag, "s"][slot] = jnp.concatenate(parts, -1).astype(BF)
+            k.send(
+                (tag, "m", slot),
+                k.buf[tag, "s"].at[slot],
+                k.buf[tag, "r"].at[slot],
+                k.dev_z(2 * sign),
+                tag,
+                k.buf[tag, "s"],
+            )
+
+        for sign in (1, -1):
+            half = 0 if sign > 0 else 1
+            add(
+                (tag, "A", sign),
+                base + 2,
+                0.3,
+                ["kvmm"],
+                [],
+                [((tag, "m", half), zlink(sign), unit), ((tag, "q", half), zlink(sign), unit)],
+                functools.partial(emit_far, sign),
+            )
+        add(
+            (tag, "C", 0),
+            base + 3,
+            0.3,
+            [(tag, "A", 1), (tag, "A", -1)],
+            [],
+            [((tag, "m", 2), ["z+"], unit), ((tag, "m", 3), ["z-"], unit)],
+            emit_near,
+        )
+        for sign in (1, -1):
+            half = 0 if sign > 0 else 1
+            add(
+                (tag, "B", sign),
+                base + 2,
+                0.2,
+                [(tag, "A", 1), (tag, "A", -1)],
+                [(tag, "m", half), (tag, "q", half)],
+                [((tag, "m", 4 + half), zlink(sign), 2 * unit)],
+                functools.partial(emit_on, sign),
+            )
+        last = [(tag, "B", 1), (tag, "B", -1), (tag, "C", 0)]
+
+        def kv_pair(t, tag):
+            total = k.pkv[t, k.z]
+            for slot in range(2, 6):
+                total = total + k.buf[tag, "r"][slot].astype(F32)
+            return total
+
+        def emit_kv_fin(t=t, tag=tag):
+            k.buf[tag + "x", "s"][...] = narrow_pair(kv_pair(t, tag))
+            k.send(tag + "x", k.buf[tag + "x", "s"], k.buf[tag + "x", "r"], k.dev_x())
+
+        add(
+            tag + "fin",
             base + 2,
-            4,
             0.2,
-            2 * R * 768,
-            counts,
-            lambda sign, s, d, t=t: k.pkv[t, d],
-            ["kvmm"],
-            lambda sign, s: [],
-            narrow_pair,
-            widen_pair,
+            last,
+            [(tag, "m", slot) for slot in range(2, 6)],
+            [(tag + "x", ["x"], 2 * R * 768)],
+            emit_kv_fin,
         )
 
-        def kv_pair(t, tag, counts):
-            return k.pkv[t, k.z] + ring_sum(tag, counts, lambda b, i: b[i], widen_pair)
-
-        def emit_kv_fin(t=t, tag=tag, counts=counts):
-            k.buf[tag + "x", "s"][...] = narrow_pair(kv_pair(t, tag, counts))
-            k.send(tag + "x", k.buf[tag + "x", "s"], k.buf[tag + "x", "r"], k.dev_x())
-
-        add(tag + "fin", base + 2, 0.2, last, last, [(tag + "x", ["x"], 2 * R * 768)], emit_kv_fin)
-
-        def emit_kv_own(t=t, tag=tag, counts=counts):
+        def emit_kv_own(t=t, tag=tag):
             k.load("tab")
-            value = kv_pair(t, tag, counts) + widen_pair(k.buf[tag + "x", "r"][...])
+            value = kv_pair(t, tag) + widen_pair(k.buf[tag + "x", "r"][...])
             for i in range(2):
                 k.kvf[t, k.z, i, :, 0:HEAD] = k.rotate(value[i, :, 0:HEAD], t, i).astype(BF)
             k.kvf[t, k.z, :, :, HEAD : 2 * HEAD] = value[:, :, HEAD : 2 * HEAD].astype(BF)
@@ -194,20 +273,43 @@
                 add(name, rank + stride * s, 0.1, after, waits, [(name, zlink(sign), size)], emit)
         return [(tag, 1, counts[0] - 1), (tag, -1, counts[1] - 1)]
 
-    kg_last = [
-        gather(
-            "kg%d" % t,
-            20 * t + 2,
-            1,
-            2 * R * 512,
-            split(1 - t),
-            lambda d, t=t: k.kvf.at[t, d],
-            ["kv%down" % t],
-            [],
-            lambda t=t: k.kvf.at[t, 0 : NZ - 1],
-        )
-        for t in range(CHUNKS)
-    ]
+    kg_waits, kg_nodes = [], []
+    for t in range(CHUNKS):
+        tag, unit = "kg%d" % t, 2 * R * 512
+
+        def emit_own_block(sign, t=t, tag=tag):
+            here = k.kvf.at[t, k.z]
+            k.send((tag, "n", sign), here, here, k.dev_z(sign))
+            k.send((tag, "f", sign), here, here, k.dev_z(2 * sign))
+
+        def emit_on_block(sign, t=t, tag=tag):
+            here = k.kvf.at[t, k.zi(-2 * sign)]
+            k.send((tag, "t", sign), here, here, k.dev_z(sign))
+            first = 0 if sign > 0 else HEAD
+            here = k.kvf.at[t, k.zi(-2 * sign), :, :, first : first + HEAD]
+            k.send((tag, "h", sign), here, here, k.dev_z(2 * sign))
+
+        for sign in (1, -1):
+            add(
+                (tag, "A", sign),
+                20 * t + 2,
+                0.2,
+                ["kv%down" % t],
+                [],
+                [((tag, "f", sign), zlink(sign), 2 * unit), ((tag, "n", sign), zlink(sign), unit)],
+                functools.partial(emit_own_block, sign),
+            )
+            add(
+                (tag, "B", sign),
+                20 * t + 2,
+                0.2,
+                [(tag, "A", sign)],
+                [(tag, "f", sign)],
+                [((tag, "t", sign), zlink(sign), unit), ((tag, "h", sign), zlink(sign), unit)],
+                functools.partial(emit_on_block, sign),
+            )
+        kg_waits.append([(tag, part, sign) for part in "nth" for sign in (1, -1)])
+        kg_nodes.append([(tag, "B", 1), (tag, "B", -1)])
 
     for t in range(CHUNKS):
         base = 40 * t
@@ -300,18 +402,10 @@
             own_nodes[c0] = tag + "own"
 
         add("mask%d" % t, base + 20, 0.3, ["kvmm"], [], [], functools.partial(lambda t: k.mask(t), t))
-        keys_in = [m for u in range(t + 1) for m in kg_last[u]]
-        keys_after = [m for u in range(t + 1) for m in ["kv%down" % u] + kg_last[u]]
+        keys_in = [m for u in range(t + 1) for m in kg_waits[u]]
+        keys_after = [m for u in range(t + 1) for m in ["kv%down" % u] + kg_nodes[u]]
         for place, (c0, width) in enumerate(ZFIRST + XFIRST):
             gtag = "g%d_%d" % (t, c0)
-
-            def emit_att(t=t, gtag=gtag, c0=c0, width=width):
-                k.attend(t, c0 // HEAD, width // HEAD)
-                here = k.att.at[t, k.z, k.xh, :, c0 : c0 + width]
-                count = NZ if (c0, width) in XFIRST else 1
-                k.send(
-                    (gtag, "x", 0), here, here, k.dev_x(), gtag + "x", k.att.at[t, 0:count, 0, :, c0 : c0 + width]
-                )
 
             add(
                 gtag + "att",
@@ -319,143 +413,172 @@
                 width / 1700.0 + 0.15,
                 [own_nodes[c0], "mask%d" % t] + keys_after,
                 keys_in,
-                [((gtag, "x", 0), ["x"], R * width * 2)],
-                emit_att,
+                [],
+                functools.partial(lambda t, first, count: k.attend(t, first, count), t, c0 // HEAD, width // HEAD),
             )
         last_step = []
-        for j, (c0, width) in enumerate(ZFIRST):
+        for j, (c0, width) in enumerate(ZFIRST + XFIRST):
             gtag = "g%d_%d" % (t, c0)
             gather(
                 gtag,
                 base + 44 + 0.1 * j,
                 4,
-                2 * R * width * 2,
-                split(j),
-                lambda d, t=t, c0=c0, width=width: k.att.at[t, d, :, :, c0 : c0 + width],
-                [gtag + "att"],
-                [(gtag, "x", 0)],
-                lambda t=t, c0=c0, width=width: k.att.at[t, 0 : NZ - 1, :, :, c0 : c0 + width],
-            )
-            last_step.append((gtag, False, split(j)))
-        for j, (c0, width) in enumerate(XFIRST):
-            gtag, counts = "g%d_%d" % (t, c0), split(j + t)
-            gather(
-                gtag,
-                base + 43,
-                4,
                 R * width * 2,
-                counts,
-                lambda d, t=t, c0=c0, width=width: k.att.at[t, d, k.xh, :, c0 : c0 + width],
+                split(j + t),
+                lambda d, t=t, c0=c0, width=width: k.att.at[t, d, :, c0 : c0 + width],
                 [gtag + "att"],
                 [],
-                lambda t=t, c0=c0, width=width: k.att.at[t, 0 : NZ - 1, 0, :, c0 : c0 + width],
-            )
-            last_step.append((gtag, True, counts))
-            for sign, n in ((1, counts[0]), (-1, counts[1])):
-                for s in range(n):
-                    name = (gtag, "x", sign, s)
-
-                    def emit_pass(t=t, gtag=gtag, sign=sign, s=s, name=name, c0=c0, width=width):
-                        here = k.att.at[t, k.zi(-sign * (s + 1)), k.xh, :, c0 : c0 + width]
-                        blocks = 1 if s == 3 else 2
-                        k.send(
-                            name,
-                            here,
-                            here,
-                            k.dev_x(),
-                            gtag + "x",
-                            k.att.at[t, 0:NZ, 0, :, c0 : c0 + width],
-                            ("pass", t, s),
-                            k.att.at[t, 0:blocks, 0, :, 0:XWIDTH],
-                        )
-
-                    after = [(gtag, sign, s + 1)] if s + 1 < n else [(gtag, sign, s)]
-                    add(
-                        name,
-                        base + 43.5 + 4 * s,
-                        0.1,
-                        after,
-                        [(gtag, sign, s)],
-                        [(name, ["x"], R * width * 2)],
-                        emit_pass,
-                    )
+                lambda t=t, c0=c0, width=width: k.att.at[t, 0 : NZ - 1, :, c0 : c0 + width],
+            )
+            last_step.append((gtag, split(j + t)))
         for rounds in OUTS[t]:
             r = rounds[-1]
             shifts, first = [], (2 * rounds[0] - 1 if rounds[0] else 0)
             waits, after = [], []
             for q in rounds:
                 shifts += [0] if q == 0 else [4] if q == 4 else [-q, q]
-                for gtag, passes, counts in last_step:
+                for gtag, counts in last_step:
                     if q == 0:
-                        waits.append((gtag, "x", 0))
                         after.append(gtag + "att")
                     for sign, n in ((1, counts[0]), (-1, counts[1])):
                         if 0 < q <= n:
                             waits.append((gtag, sign, q - 1))
                             after.append((gtag, sign, q - 1))
-                            if passes:
-                                waits.append((gtag, "x", sign, q - 1))
-                                after.append((gtag, "x", sign, q - 1))
-
-            def emit_out(t=t, r=r, shifts=shifts, first=first):
-                k.load("wout")
-                count = len(shifts)
-                rows = [k.att[t, k.zi(s)].reshape(2 * R, QCOLS) for s in shifts]
-                lhs = rows[0] if count == 1 else jnp.concatenate(rows, 0)
-                for delta in (2, 1, 3, 0):
-                    c0 = pl.multiple_of(lax.rem(k.y + delta, NY) * 256, 256)
-                    res = jnp.dot(lhs, k.wout[:, pl.ds(c0, 256)], preferred_element_type=F32)
-                    res = res.reshape(count, 2 * R, 256)
-                    if delta == 0:
-                        k.oown[t, first : first + count] = res
-                    else:
-                        k.ys[t, delta - 1, first : first + count] = res.astype(BF)
-                        k.send(
-                            ("y", t, r, delta),
-                            k.ys.at[t, delta - 1, first : first + count],
-                            k.yr.at[t, delta - 1, first : first + count],
-                            k.dev_y(delta),
-                            "y",
-                            k.ys,
-                            ("y", t, r),
-                            k.yr.at[t, :, first : first + count],
-                        )
-
-            size = len(shifts) * 2 * R * 512
+            for half in range(2):
+                if half:
+                    after = after + [("wo", "d", p) for p in range(PIECES)]
+                    waits = waits + [("wo", leg, p) for leg in ("d", "e") for p in range(PIECES)]
+
+                def emit_out(t=t, r=r, half=half, shifts=shifts, first=first):
+                    k.load("wout")
+                    count = len(shifts)
+                    rows = [k.att[t, k.zi(s)] for s in shifts]
+                    lhs = rows[0] if count == 1 else jnp.concatenate(rows, 0)
+                    weights = k.wother if half else k.wout
+                    for delta in (2, 1, 3, 0):
+                        c0 = pl.multiple_of(lax.rem(k.y + delta, NY) * 256, 256)
+                        res = jnp.dot(lhs, weights[:, pl.ds(c0, 256)], preferred_element_type=F32)
+                        res = res.reshape(count, R, 256)
+                        if delta == 0:
+                            k.oown[half, t, first : first + count] = res
+                        else:
+                            k.ys[half, t, delta - 1, first : first + count] = res.astype(BF)
+                            k.send(
+                                ("y", t, r, half, delta),
+                                k.ys.at[half, t, delta - 1, first : first + count],
+                                k.yr.at[half, t, delta - 1, first : first + count],
+                                k.dev_y(delta),
+                                "y",
+                                k.ys,
+                                ("y", t, r, half),
+                                k.yr.at[half, t, :, first : first + count],
+                            )
+
+                size = len(shifts) * R * 512
+                add(
+                    ("out", t, r, half),
+                    base + 45 + 4 * r,
+                    0.75 + 0.0012 * R * len(shifts),
+                    after,
+                    waits,
+                    [
+                        (("y", t, r, half, 2), ["y+", "y-"], size),
+                        (("y", t, r, half, 1), ["y+"], size),
+                        (("y", t, r, half, 3), ["y-"], size),
+                    ],
+                    emit_out,
+                )
+
+                def put(t, shift, half, value):
+                    row = pl.multiple_of(t * ROWS + (k.zi(shift) * 2 + half) * R, R)
+                    k.out[pl.ds(row, R), :] = value
+
+                def emit_fin(t=t, r=r, half=half, shifts=shifts, first=first):
+                    for i, shift in enumerate(shifts):
+                        total = k.oown[half, t, first + i]
+                        for delta in range(NY - 1):
+                            total = total + k.yr[half, t, delta, first + i].astype(F32)
+                        if half:
+                            k.xs[t, first + i] = total.astype(BF)
+                        else:
+                            put(t, shift, k.xh, total.astype(BF))
+                    if half:
+                        slots = slice(first, first + len(shifts))
+                        k.send(("xo", t, r), k.xs.at[t, slots], k.xr.at[t, slots], k.dev_x(), "xo", k.xs)
+
+                add(
+                    ("fin", t, r, half),
+                    base + 50 + 4 * r,
+                    0.15 + 0.03 * len(shifts),
+                    [("out", t, r, half)],
+                    [("y", t, r, half, delta) for delta in (1, 2, 3)],
+                    [(("xo", t, r), ["x"], len(shifts) * R * 512)] if half else [],
+                    emit_fin,
+                )
+
+            def emit_in(t=t, shifts=shifts, first=first):
+                for i, shift in enumerate(shifts):
+                    put(t, shift, 1 - k.xh, k.xr[t, first + i])
+
             add(
-                ("out", t, r),
-                base + 45 + 4 * r,
-                0.55 + 0.15 + 0.0024 * 2 * R * len(shifts),
-                after,
-                waits,
-                [(("y", t, r, 2), ["y+", "y-"], size), (("y", t, r, 1), ["y+"], size), (("y", t, r, 3), ["y-"], size)],
-                emit_out,
-            )
-
-            def emit_fin(t=t, shifts=shifts, first=first):
-                for i, shift in enumerate(shifts):
-                    total = k.oown[t, first + i]
-                    for delta in range(NY - 1):
-                        total = total + k.yr[t, delta, first + i].astype(F32)
-                    row = pl.multiple_of(t * ROWS + k.zi(shift) * 2 * R, 2 * R)
-                    k.out[pl.ds(row, 2 * R), :] = total
-
-            add(
-                ("fin", t, r),
-                base + 50 + 4 * r,
-                0.15 + 0.05 * len(shifts),
-                [("out", t, r)],
-                [("y", t, r, delta) for delta in (1, 2, 3)],
-                [],
-                emit_fin,
-            )
+                ("in", t, r), base + 54 + 4 * r, 0.1 + 0.02 * len(shifts), [("fin", t, r, 1)], [("xo", t, r)], [], emit_in
+            )
+
+    def quarter(owner, p):
+        return pl.ds(pl.multiple_of(owner * QUARTER + p * PIECE, PIECE), PIECE)
+
+    size = PIECE * OCOLS * 2
+    for p in range(PIECES):
+
+        def emit_cross(p=p):
+            k.load("wout")
+            k.send(
+                ("wo", "c", p),
+                k.wout.at[quarter(k.dp, p)],
+                k.wother.at[quarter(k.dp, p)],
+                k.dev_cross(),
+                "woc",
+                k.wother.at[0:QUARTER],
+            )
+
+        add(("wo", "c", p), 12 + p, 0.12, ["kvmm"], [], [(("wo", "c", p), ["x"], size // 2)], emit_cross)
+
+        def emit_inner(p=p):
+            here = k.wother.at[quarter(k.dp_cross, p)]
+            k.send(("wo", "i", p), here, here, k.dev_inner(), "woi", k.wother.at[0:QUARTER])
+            k.send(("wo", "d", p), here, here, k.dev_core(), "wod", k.wother.at[0:QUARTER])
+
+        add(
+            ("wo", "i", p),
+            18 + p,
+            0.2,
+            [("wo", "c", p)],
+            [("wo", "c", p)],
+            [(("wo", "i", p), ["x"], size // 2), (("wo", "d", p), ["c"], size // 7)],
+            emit_inner,
+        )
+
+        def emit_core(p=p):
+            here = k.wother.at[quarter(k.dp_core, p)]
+            k.send(("wo", "e", p), here, here, k.dev_core(), "woe", k.wother.at[0:QUARTER])
+
+        add(
+            ("wo", "d", p),
+            24 + p,
+            0.12,
+            [("wo", "i", p)],
+            [("wo", "i", p)],
+            [(("wo", "e", p), ["c"], size // 7)],
+            emit_core,
+        )
     return nodes
 
 
 def buffers():
     shapes = {}
     for t in range(CHUNKS):
-        shapes["kv%d" % t] = (7, 2, R, 384)
+        shapes["kv%d" % t] = (6, 2, R, 256)
+        shapes["kv%dq" % t] = (2, 2, R, 128)
         shapes["kv%dx" % t] = (2, R, 384)
         for c0, width in ZFIRST:
             shapes["zf%d_%d" % (t, c0)] = (7, 2, R, width)
@@ -473,7 +596,8 @@
 def kernel(order_names, messages, *refs):
     shapes = buffers()
     names = ["docs", "h_tok", "h_wq", "h_wk", "h_wv", "h_wout", "h_tab", "out"]
-    names += ["tok", "wq", "wkv", "wout", "tab", "bias", "pq", "pkv", "kvf", "qs", "att", "oown", "ys", "yr"]
+    names += ["tok", "wq", "wkv", "wout", "wother", "tab", "bias", "pq", "pkv", "kvf", "qs", "att"]
+    names += ["oown", "ys", "yr", "xs", "xr"]
     k = Kernel()
     for name, ref in zip(names, refs):
         setattr(k, name, ref)
@@ -489,10 +613,18 @@
     k.dev_z = lambda sign: {"loop": k.xh * NZ + k.zi(sign)}
     k.dev_x = lambda: {"loop": (1 - k.xh) * NZ + k.z}
     k.dev_y = lambda delta: {"column": lax.rem(k.y + delta, NY)}
+    k.dp = lax.axis_index("dp")
+    other_chip = lax.rem(k.dp + 2, 4)
+    other_core = k.dp + 1 - 2 * lax.rem(k.dp, 2)
+    k.dp_cross, k.dp_core = other_chip, k.dp
+    k.dev_cross = lambda: {"loop": (1 - k.xh) * NZ + k.z, "dp": other_chip}
+    k.dev_inner = lambda: {"dp": other_chip}
+    k.dev_core = lambda: {"dp": other_core}
     mesh_id = pl.DeviceIdType.MESH
 
     barrier = pltpu.get_barrier_semaphore()
-    peers = [k.dev_z(1), k.dev_z(-1), k.dev_x()] + [k.dev_y(delta) for delta in (1, 2, 3)]
+    peers = [k.dev_z(1), k.dev_z(-1), k.dev_z(2), k.dev_z(-2), k.dev_x(), k.dev_cross(), k.dev_inner(), k.dev_core()]
+    peers += [k.dev_y(delta) for delta in (1, 2, 3)]
     for peer in peers:
         pl.semaphore_signal(barrier, inc=1, device_id=peer, device_id_type=mesh_id)
 
@@ -602,7 +734,7 @@
         mixed = (mixed.reshape(count, R, HEAD) / total).astype(BF)
         for i in range(count):
             c0 = (first + i) * HEAD
-            k.att[t, k.z, k.xh, :, c0 : c0 + HEAD] = mixed[i]
+            k.att[t, k.z, :, c0 : c0 + HEAD] = mixed[i]
 
     k.attend = attend
 
@@ -627,11 +759,17 @@
         if isinstance(name, tuple):
             tag = name[0]
             if tag == "y":
-                group, receive = "y", name[:3]
+                group, receive = "y", name[:4]
+            elif tag == "wo":
+                group = tag + name[1]
+            elif tag[:2] == "kv" and name[1] == "q":
+                group = tag + "q"
+            elif tag[:2] == "kg":
+                group = name
+            elif tag == "xo":
+                group = tag
             elif name[1] == "x":
                 group = tag + "x"
-                if len(name) == 4:
-                    receive = ("pass", tag[:2], name[3])
             else:
                 group = tag
         sends.add(group)
@@ -649,16 +787,19 @@
         pltpu.VMEM((MODEL, QCOLS), BF),
         pltpu.VMEM((MODEL, 2 * HEAD), BF),
         pltpu.VMEM((QCOLS, OCOLS), BF),
+        pltpu.VMEM((QCOLS, OCOLS), BF),
         pltpu.VMEM((CHUNKS, 2, R, 2 * HEAD), F32),
         pltpu.VMEM((CHUNKS, R, SEQ), F32),
         pltpu.VMEM((CHUNKS, NZ, 2, R, QCOLS), F32),
         pltpu.VMEM((CHUNKS, NZ, 2, R, 2 * HEAD), F32),
         pltpu.VMEM((CHUNKS, NZ, 2, R, 2 * HEAD), BF),
         pltpu.VMEM((CHUNKS, QCOLS // HEAD, R, HEAD), BF),
-        pltpu.VMEM((CHUNKS, NZ, 2, R, QCOLS), BF),
-        pltpu.VMEM((CHUNKS, NZ, 2 * R, 256), F32),
-        pltpu.VMEM((CHUNKS, NY - 1, NZ, 2 * R, 256), BF),
-        pltpu.VMEM((CHUNKS, NY - 1, NZ, 2 * R, 256), BF),
+        pltpu.VMEM((CHUNKS, NZ, R, QCOLS), BF),
+        pltpu.VMEM((2, CHUNKS, NZ, R, 256), F32),
+        pltpu.VMEM((2, CHUNKS, NY - 1, NZ, R, 256), BF),
+        pltpu.VMEM((2, CHUNKS, NY - 1, NZ, R, 256), BF),
+        pltpu.VMEM((CHUNKS, NZ, R, 256), BF),
+        pltpu.VMEM((CHUNKS, NZ, R, 256), BF),
     ]
     for shape in buffers().values():
         scratch += [pltpu.VMEM(shape, BF), pltpu.VMEM(shape, BF)]
@@ -671,7 +812,7 @@
     vmem = pl.BlockSpec(memory_space=pltpu.VMEM)
     return pl.pallas_call(
         functools.partial(kernel, [node.name for node in order], messages),
-        out_shape=jax.ShapeDtypeStruct((SEQ, 256), F32),
+        out_shape=jax.ShapeDtypeStruct((SEQ, 256), BF),
         in_specs=[vmem] + [anywhere] * 6,
         out_specs=vmem,
         scratch_shapes=scratch,
@@ -679,7 +820,7 @@
             collective_id=0, has_side_effects=True, vmem_limit_bytes=56 * 1024 * 1024
         ),
         name="sublayer",
-    )(doc_ids.reshape(1, SEQ), tokens, w_query, key_weight, value_weight, w_out, jnp.asarray(rotary_table())).astype(BF)
+    )(doc_ids.reshape(1, SEQ), tokens, w_query, key_weight, value_weight, w_out, jnp.asarray(rotary_table()))
 
 
 def solution(mesh):

time: 97.1 us -> 123 us (1.27)
  Pallas kernels: 94.7 us -> 121 us
  other arithmetic: 2.07 us -> 0 us
  local copies, waits for them, and re-layouts: 0 us -> 1.87 us
    pallas_call x1, Pallas kernels: 94.7 us -> 121 us  [shards(): pl.pallas_call(functools.partial(kernel, [node.name for node in order], m...]
    convert_element_type x1 -> x0, other arithmetic: 2.07 us -> none  [shards(): return pl.pallas_call(functools.partial(kernel, [node.name for node in or...]
    unnamed x0 -> x1, local copies, waits for them, and re-layouts: none -> 1.87 us
where the time goes in v3:
time: 123 us
  Pallas kernels  121 us (98%)
  local copies, waits for them, and re-layouts  1.87 us (2%)
    pallas_call x1, Pallas kernels, shards(): pl.pallas_call(functools.partial(kernel, [node.name for node in order], m...  121 us

profile of v3, /device:TPU:2, one launch (start us, length us, event | category | flops | bytes accessed | tf_op | source)
XLA Modules:
  0.0 123.1 jit_solution(6975380269957582942)
XLA Ops:
  0.0 121.2 %sublayer.1 = bf16[1024,256]{1,0:T(8,128)(2,1)} custom-call(s32[1,1024]{1,0:T(1,128)} %bitcast.1, bf16[1024,1024]{1,0:T(8,128)(2,1)} %refs_1_.1, bf16[1024,2048]{1,0:T(8,128)(2,1)} %refs_2_.1, bf16[1024,128]{1,0:T(8,128)(2,1)} %refs_3_.1, bf16[1024,128]{1,0:T(8,128)(2,1)} %refs_4_.1, bf16[2048,1024]{1,0:T(8,128)(2,1)} %refs_5_.1, ...), custom_call_target="tpu_custom_call" | custom-call | tf_op jit(solution)/shard_map/sublayer/pallas_call | solution.py:813
  121.2 1.9 %copy.9 = bf16[1024,256]{1,0:T(8,128)(2,1)} copy(bf16[1024,256]{1,0:T(8,128)(2,1)} %sublayer.1) | data formatting | bytes 1048576

commit v4 on v2

--- a/solution.py
+++ b/solution.py
@@ -19,24 +19,24 @@
 CHUNKS = 2
 ROWS = SEQ // CHUNKS
 R = ROWS // (2 * NZ)
-XFIRST = ((0, 768), (768, 640))
-ZFIRST = ((1408, 640),)
-QUERY_PARTS = (2, 3, 0, 1)
-XWIDTH = sum(width for _, width in XFIRST)
+XFIRST = (((0, 768), (768, 640)), ((0, 768), (768, 640)))
+ZFIRST = (((1408, 640),), ((1408, 640),))
+QUERY_PARTS = (1, 2, 3, 0)
+XWIDTH = tuple(sum(width for _, width in streams) for streams in XFIRST)
 OUTS = (((0,), (1,), (2,), (3,), (4,)), ((0,), (1,), (2,), (3,), (4,)))
 BF = jnp.bfloat16
 F32 = jnp.float32
 SCALE = math.log2(math.e) / math.sqrt(HEAD)
 ORDER = (
-    0, 11, 7, 3, 64, 16, 70, 19, 1, 39, 67, 43, 12, 8, 69, 68, 66, 65, 17, 2, 53, 4, 20, 40, 133, 54, 9, 71, 21,
-    49, 48, 13, 129, 51, 80, 44, 10, 72, 18, 75, 41, 22, 5, 14, 50, 170, 139, 52, 55, 60, 56, 134, 6, 155, 45, 23,
-    42, 130, 15, 144, 28, 158, 138, 61, 154, 25, 57, 73, 143, 76, 29, 62, 46, 157, 141, 156, 161, 24, 160, 159, 26,
-    58, 165, 32, 36, 131, 140, 74, 142, 145, 30, 77, 135, 37, 59, 27, 149, 47, 33, 146, 166, 31, 132, 78, 63, 162,
-    34, 150, 82, 95, 91, 79, 167, 163, 136, 151, 147, 83, 38, 81, 35, 164, 168, 96, 102, 152, 108, 148, 105, 92,
-    137, 98, 171, 169, 173, 198, 84, 153, 172, 184, 106, 181, 109, 112, 97, 115, 195, 103, 119, 199, 93, 185, 174,
-    191, 107, 88, 110, 104, 182, 99, 178, 209, 113, 200, 205, 186, 120, 188, 196, 85, 89, 175, 202, 111, 94, 117,
-    116, 179, 114, 206, 100, 192, 201, 183, 187, 197, 203, 121, 86, 90, 176, 189, 207, 211, 180, 193, 204, 190,
-    123, 194, 101, 208, 118, 87, 125, 177, 213, 215, 217, 127, 212, 126, 122, 214, 210, 218, 124, 216, 128,
+    0, 1, 12, 8, 4, 65, 17, 71, 20, 2, 40, 68, 44, 13, 9, 70, 69, 67, 66, 18, 3, 54, 5, 21, 41, 134, 55, 10, 72,
+    22, 50, 49, 14, 130, 52, 81, 45, 11, 73, 19, 76, 42, 23, 6, 15, 51, 171, 140, 53, 56, 61, 57, 135, 7, 156, 46,
+    24, 43, 131, 16, 145, 29, 159, 139, 62, 155, 26, 58, 74, 144, 77, 30, 63, 47, 158, 142, 157, 162, 25, 161, 160,
+    27, 59, 166, 33, 37, 132, 141, 75, 143, 146, 31, 78, 136, 38, 60, 28, 150, 48, 34, 147, 167, 32, 133, 79, 64,
+    163, 35, 151, 83, 96, 92, 80, 168, 164, 137, 152, 148, 84, 39, 82, 36, 165, 169, 97, 103, 153, 109, 149, 106,
+    93, 138, 99, 172, 170, 174, 199, 85, 154, 173, 185, 107, 182, 110, 113, 98, 116, 196, 104, 120, 200, 94, 186,
+    175, 192, 108, 89, 111, 105, 183, 100, 179, 210, 114, 201, 206, 187, 121, 189, 197, 86, 90, 176, 203, 112, 95,
+    118, 117, 180, 115, 207, 101, 193, 202, 184, 188, 198, 204, 122, 87, 91, 177, 190, 208, 212, 181, 194, 205,
+    191, 124, 195, 102, 209, 119, 88, 126, 178, 214, 216, 218, 128, 213, 127, 123, 215, 211, 219, 125, 217, 129,
 )
 
 
@@ -88,16 +88,18 @@
     def zlink(sign):
         return ["z+"] if sign > 0 else ["z-"]
 
-    def emit_kv():
+    def emit_kv(t):
         k.load("wkv")
-        for t in range(CHUNKS):
-            k.load("tok%d" % t)
-            res = jnp.dot(k.tok[pl.ds(t * ROWS, ROWS)], k.wkv[...], preferred_element_type=F32)
-            k.pkv[t] = res.reshape(NZ, 2, R, 2 * HEAD)
-        k.query_loads()
-        k.ready()
-
-    add("kvmm", 0, 4.0, [], [], [], emit_kv)
+        k.load("tok%d" % t)
+        if t == 0:
+            k.query_loads()
+        res = jnp.dot(k.tok[pl.ds(t * ROWS, ROWS)], k.wkv[...], preferred_element_type=F32)
+        k.pkv[t] = res.reshape(NZ, 2, R, 2 * HEAD)
+        if t == 0:
+            k.ready()
+
+    for t in range(CHUNKS):
+        add("kvmm%d" % t, t, 0.5 if t else 3.4, ["kvmm0"] if t else [], [], [], functools.partial(emit_kv, t))
 
     def emit_q(t, c0, width):
         for c in range(c0 // 512, (c0 + width - 1) // 512 + 1):
@@ -109,12 +111,12 @@
             k.last_loads = None
 
     for t in range(CHUNKS):
-        for c0, width in ZFIRST + XFIRST:
+        for c0, width in ZFIRST[t] + XFIRST[t]:
             add(
                 "q%d_%d" % (t, c0),
-                1 + t * 40 + (0.1 if c0 < ZFIRST[0][0] else 0),
+                1 + t * 40 + (0.1 if c0 < ZFIRST[t][0][0] else 0),
                 width / 620.0,
-                ["kvmm"],
+                ["kvmm%d" % t],
                 [],
                 [],
                 functools.partial(emit_q, t, c0, width),
@@ -156,7 +158,7 @@
             2 * R * 768,
             counts,
             lambda sign, s, d, t=t: k.pkv[t, d],
-            ["kvmm"],
+            ["kvmm%d" % t],
             lambda sign, s: [],
             narrow_pair,
             widen_pair,
@@ -212,7 +214,7 @@
     for t in range(CHUNKS):
         base = 40 * t
         own_nodes = {}
-        for j, (c0, width) in enumerate(ZFIRST):
+        for j, (c0, width) in enumerate(ZFIRST[t]):
             tag, counts = "zf%d_%d" % (t, c0), split(j)
             last = ring(
                 tag,
@@ -242,7 +244,7 @@
             add(tag + "own", base + 37, 0.25, [tag + "fin"], [tag + "x"], [], emit_own)
             own_nodes[c0] = tag + "own"
 
-        for j, (c0, width) in enumerate(XFIRST):
+        for j, (c0, width) in enumerate(XFIRST[t]):
             tag, counts = "xf%d_%d" % (t, c0), split(j + t)
             slots = [(1, s) for s in range(counts[0])] + [(-1, s) for s in range(counts[1])] + [(0, 0)]
             queue = sorted(range(NZ), key=lambda i, slots=slots: (slots[i][1] if slots[i][0] else 9, i))
@@ -299,16 +301,16 @@
             add(tag + "own", base + 37.5, 0.25, last, last + [(tag, "x", NZ - 1)], [], emit_xf_own)
             own_nodes[c0] = tag + "own"
 
-        add("mask%d" % t, base + 20, 0.3, ["kvmm"], [], [], functools.partial(lambda t: k.mask(t), t))
+        add("mask%d" % t, base + 20, 0.3, ["kvmm0"], [], [], functools.partial(lambda t: k.mask(t), t))
         keys_in = [m for u in range(t + 1) for m in kg_last[u]]
         keys_after = [m for u in range(t + 1) for m in ["kv%down" % u] + kg_last[u]]
-        for place, (c0, width) in enumerate(ZFIRST + XFIRST):
+        for place, (c0, width) in enumerate(ZFIRST[t] + XFIRST[t]):
             gtag = "g%d_%d" % (t, c0)
 
             def emit_att(t=t, gtag=gtag, c0=c0, width=width):
                 k.attend(t, c0 // HEAD, width // HEAD)
                 here = k.att.at[t, k.z, k.xh, :, c0 : c0 + width]
-                count = NZ if (c0, width) in XFIRST else 1
+                count = NZ if (c0, width) in XFIRST[t] else 1
                 k.send(
                     (gtag, "x", 0), here, here, k.dev_x(), gtag + "x", k.att.at[t, 0:count, 0, :, c0 : c0 + width]
                 )
@@ -323,7 +325,7 @@
                 emit_att,
             )
         last_step = []
-        for j, (c0, width) in enumerate(ZFIRST):
+        for j, (c0, width) in enumerate(ZFIRST[t]):
             gtag = "g%d_%d" % (t, c0)
             gather(
                 gtag,
@@ -337,7 +339,7 @@
                 lambda t=t, c0=c0, width=width: k.att.at[t, 0 : NZ - 1, :, :, c0 : c0 + width],
             )
             last_step.append((gtag, False, split(j)))
-        for j, (c0, width) in enumerate(XFIRST):
+        for j, (c0, width) in enumerate(XFIRST[t]):
             gtag, counts = "g%d_%d" % (t, c0), split(j + t)
             gather(
                 gtag,
@@ -366,7 +368,7 @@
                             gtag + "x",
                             k.att.at[t, 0:NZ, 0, :, c0 : c0 + width],
                             ("pass", t, s),
-                            k.att.at[t, 0:blocks, 0, :, 0:XWIDTH],
+                            k.att.at[t, 0:blocks, 0, :, 0 : XWIDTH[t]],
                         )
 
                     after = [(gtag, sign, s + 1)] if s + 1 < n else [(gtag, sign, s)]
@@ -438,7 +440,7 @@
                     for delta in range(NY - 1):
                         total = total + k.yr[t, delta, first + i].astype(F32)
                     row = pl.multiple_of(t * ROWS + k.zi(shift) * 2 * R, 2 * R)
-                    k.out[pl.ds(row, 2 * R), :] = total
+                    k.out[pl.ds(row, 2 * R), :] = total.astype(BF)
 
             add(
                 ("fin", t, r),
@@ -457,10 +459,10 @@
     for t in range(CHUNKS):
         shapes["kv%d" % t] = (7, 2, R, 384)
         shapes["kv%dx" % t] = (2, R, 384)
-        for c0, width in ZFIRST:
+        for c0, width in ZFIRST[t]:
             shapes["zf%d_%d" % (t, c0)] = (7, 2, R, width)
             shapes["zf%d_%dx" % (t, c0)] = (R, width)
-        for c0, width in XFIRST:
+        for c0, width in XFIRST[t]:
             shapes["xf%d_%d" % (t, c0)] = (7, R, width)
             shapes["xf%d_%dx" % (t, c0)] = (8, R, width)
     return shapes
@@ -671,7 +673,7 @@
     vmem = pl.BlockSpec(memory_space=pltpu.VMEM)
     return pl.pallas_call(
         functools.partial(kernel, [node.name for node in order], messages),
-        out_shape=jax.ShapeDtypeStruct((SEQ, 256), F32),
+        out_shape=jax.ShapeDtypeStruct((SEQ, 256), BF),
         in_specs=[vmem] + [anywhere] * 6,
         out_specs=vmem,
         scratch_shapes=scratch,
@@ -679,7 +681,7 @@
             collective_id=0, has_side_effects=True, vmem_limit_bytes=56 * 1024 * 1024
         ),
         name="sublayer",
-    )(doc_ids.reshape(1, SEQ), tokens, w_query, key_weight, value_weight, w_out, jnp.asarray(rotary_table())).astype(BF)
+    )(doc_ids.reshape(1, SEQ), tokens, w_query, key_weight, value_weight, w_out, jnp.asarray(rotary_table()))
 
 
 def solution(mesh):

time: 97.1 us -> 95.6 us (0.985)
  other arithmetic: 2.07 us -> 0 us
  local copies, waits for them, and re-layouts: 0 us -> 1.87 us
  Pallas kernels: 94.7 us -> 93.5 us
    convert_element_type x1 -> x0, other arithmetic: 2.07 us -> none  [shards(): return pl.pallas_call(functools.partial(kernel, [node.name for node in or...]
    unnamed x0 -> x1, local copies, waits for them, and re-layouts: none -> 1.87 us
    pallas_call x1, Pallas kernels: 94.7 us -> 93.5 us  [shards(): pl.pallas_call(functools.partial(kernel, [node.name for node in order], m...]
where the time goes in v4:
time: 95.6 us; the launch traced here: 95.4 us
  Pallas kernels  93.5 us (98%)
  local copies, waits for them, and re-layouts  1.87 us (2%)
    pallas_call x1, Pallas kernels, shards(): pl.pallas_call(functools.partial(kernel, [node.name for node in order], m...  93.5 us

profile of v4, /device:TPU:2, one launch (start us, length us, event | category | flops | bytes accessed | tf_op | source)
XLA Modules:
  0.0 95.4 jit_solution(15772487013203082184)
XLA Ops:
  0.0 93.5 %sublayer.1 = bf16[1024,256]{1,0:T(8,128)(2,1)} custom-call(s32[1,1024]{1,0:T(1,128)} %bitcast.1, bf16[1024,1024]{1,0:T(8,128)(2,1)} %refs_1_.1, bf16[1024,2048]{1,0:T(8,128)(2,1)} %refs_2_.1, bf16[1024,128]{1,0:T(8,128)(2,1)} %refs_3_.1, bf16[1024,128]{1,0:T(8,128)(2,1)} %refs_4_.1, bf16[2048,1024]{1,0:T(8,128)(2,1)} %refs_5_.1, ...), custom_call_target="tpu_custom_call" | custom-call | tf_op jit(solution)/shard_map/sublayer/pallas_call | solution.py:674
  93.5 1.9 %copy.9 = bf16[1024,256]{1,0:T(8,128)(2,1)} copy(bf16[1024,256]{1,0:T(8,128)(2,1)} %sublayer.1) | data formatting | bytes 1048576

commit v5 on v4

--- a/solution.py
+++ b/solution.py
@@ -19,24 +19,25 @@
 CHUNKS = 2
 ROWS = SEQ // CHUNKS
 R = ROWS // (2 * NZ)
-XFIRST = (((0, 768), (768, 640)), ((0, 768), (768, 640)))
-ZFIRST = (((1408, 640),), ((1408, 640),))
-QUERY_PARTS = (1, 2, 3, 0)
+XFIRST = (((0, 768), (768, 640)), ((0, 640), (640, 640)))
+ZFIRST = (((1408, 640),), ((1280, 384), (1664, 384)))
+QUERY_PARTS = (2, 3, 0, 1)
 XWIDTH = tuple(sum(width for _, width in streams) for streams in XFIRST)
 OUTS = (((0,), (1,), (2,), (3,), (4,)), ((0,), (1,), (2,), (3,), (4,)))
 BF = jnp.bfloat16
 F32 = jnp.float32
 SCALE = math.log2(math.e) / math.sqrt(HEAD)
 ORDER = (
-    0, 1, 12, 8, 4, 65, 17, 71, 20, 2, 40, 68, 44, 13, 9, 70, 69, 67, 66, 18, 3, 54, 5, 21, 41, 134, 55, 10, 72,
-    22, 50, 49, 14, 130, 52, 81, 45, 11, 73, 19, 76, 42, 23, 6, 15, 51, 171, 140, 53, 56, 61, 57, 135, 7, 156, 46,
-    24, 43, 131, 16, 145, 29, 159, 139, 62, 155, 26, 58, 74, 144, 77, 30, 63, 47, 158, 142, 157, 162, 25, 161, 160,
-    27, 59, 166, 33, 37, 132, 141, 75, 143, 146, 31, 78, 136, 38, 60, 28, 150, 48, 34, 147, 167, 32, 133, 79, 64,
-    163, 35, 151, 83, 96, 92, 80, 168, 164, 137, 152, 148, 84, 39, 82, 36, 165, 169, 97, 103, 153, 109, 149, 106,
-    93, 138, 99, 172, 170, 174, 199, 85, 154, 173, 185, 107, 182, 110, 113, 98, 116, 196, 104, 120, 200, 94, 186,
-    175, 192, 108, 89, 111, 105, 183, 100, 179, 210, 114, 201, 206, 187, 121, 189, 197, 86, 90, 176, 203, 112, 95,
-    118, 117, 180, 115, 207, 101, 193, 202, 184, 188, 198, 204, 122, 87, 91, 177, 190, 208, 212, 181, 194, 205,
-    191, 124, 195, 102, 209, 119, 88, 126, 178, 214, 216, 218, 128, 213, 127, 123, 215, 211, 219, 125, 217, 129,
+    0, 9, 13, 1, 18, 5, 21, 135, 131, 3, 51, 6, 55, 10, 14, 56, 54, 140, 143, 19, 53, 22, 2, 132, 45, 4, 41, 52,
+    11, 144, 15, 71, 50, 7, 8, 66, 23, 57, 168, 42, 152, 46, 20, 12, 133, 24, 136, 145, 58, 141, 62, 82, 16, 43,
+    67, 25, 69, 72, 47, 166, 73, 165, 68, 59, 150, 154, 17, 149, 167, 30, 70, 27, 170, 74, 77, 63, 169, 26, 172,
+    171, 34, 151, 38, 176, 142, 155, 28, 153, 31, 156, 44, 78, 137, 134, 146, 173, 75, 35, 160, 60, 39, 32, 29, 79,
+    181, 161, 177, 48, 157, 174, 76, 40, 80, 36, 147, 64, 33, 61, 138, 81, 37, 178, 162, 158, 85, 175, 65, 49, 83,
+    84, 179, 139, 97, 107, 159, 182, 93, 110, 148, 163, 183, 180, 185, 217, 214, 111, 108, 164, 94, 184, 200, 100,
+    203, 98, 117, 121, 114, 86, 104, 90, 218, 215, 112, 186, 221, 224, 204, 95, 101, 109, 99, 201, 105, 210, 193,
+    196, 190, 87, 207, 115, 91, 219, 187, 225, 205, 216, 113, 96, 118, 102, 123, 197, 106, 202, 116, 191, 119, 194,
+    208, 211, 88, 92, 222, 230, 220, 122, 188, 223, 206, 226, 228, 198, 212, 209, 125, 195, 120, 192, 103, 89, 127,
+    189, 227, 213, 232, 199, 234, 129, 236, 233, 229, 126, 124, 235, 128, 231, 130, 237,
 )
 
 
@@ -673,7 +674,7 @@
     vmem = pl.BlockSpec(memory_space=pltpu.VMEM)
     return pl.pallas_call(
         functools.partial(kernel, [node.name for node in order], messages),
-        out_shape=jax.ShapeDtypeStruct((SEQ, 256), BF),
+        out_shape=pltpu.VMEM((SEQ, 256), BF),
         in_specs=[vmem] + [anywhere] * 6,
         out_specs=vmem,
         scratch_shapes=scratch,

time: 95.6 us -> 94.1 us (0.984)
  local copies, waits for them, and re-layouts: 1.87 us -> 0.8 us
    unnamed x1, local copies, waits for them, and re-layouts: 1.87 us -> 0.8 us
where the time goes in v5:
time: 94.1 us; the launch traced here: 93.9 us
  Pallas kernels  93.1 us (99%)
    pallas_call x1, Pallas kernels, shards(): pl.pallas_call(functools.partial(kernel, [node.name for node in order], m...  93.1 us

profile of v5, /device:TPU:2, one launch (start us, length us, event | category | flops | bytes accessed | tf_op | source)
XLA Modules:
  0.0 93.9 jit_solution(3322624525625496491)
XLA Ops:
  0.0 93.1 %sublayer.1 = bf16[1024,256]{1,0:T(8,128)(2,1)S(1)} custom-call(s32[1,1024]{1,0:T(1,128)} %bitcast.1, bf16[1024,1024]{1,0:T(8,128)(2,1)} %refs_1_.1, bf16[1024,2048]{1,0:T(8,128)(2,1)} %refs_2_.1, bf16[1024,128]{1,0:T(8,128)(2,1)} %refs_3_.1, bf16[1024,128]{1,0:T(8,128)(2,1)} %refs_4_.1, bf16[2048,1024]{1,0:T(8,128)(2,1)} %refs_5_.1, ...), custom_call_target="tpu_custom_call" | custom-call | tf_op jit(solution)/shard_map/sublayer/pallas_call | solution.py:675
  93.1 0.8 copy.9

commit v6 on v5

--- a/solution.py
+++ b/solution.py
@@ -90,10 +90,10 @@
         return ["z+"] if sign > 0 else ["z-"]
 
     def emit_kv(t):
+        if t == 0:
+            k.query_loads()
         k.load("wkv")
         k.load("tok%d" % t)
-        if t == 0:
-            k.query_loads()
         res = jnp.dot(k.tok[pl.ds(t * ROWS, ROWS)], k.wkv[...], preferred_element_type=F32)
         k.pkv[t] = res.reshape(NZ, 2, R, 2 * HEAD)
         if t == 0:
@@ -107,9 +107,6 @@
             k.load("wq%d" % c)
         res = jnp.dot(k.tok[pl.ds(t * ROWS, ROWS)], k.wq[:, c0 : c0 + width], preferred_element_type=F32)
         k.pq[t, :, :, :, c0 : c0 + width] = res.reshape(NZ, 2, R, width)
-        if k.last_loads:
-            k.last_loads()
-            k.last_loads = None
 
     for t in range(CHUNKS):
         for c0, width in ZFIRST[t] + XFIRST[t]:
@@ -169,6 +166,9 @@
             return k.pkv[t, k.z] + ring_sum(tag, counts, lambda b, i: b[i], widen_pair)
 
         def emit_kv_fin(t=t, tag=tag, counts=counts):
+            if k.last_loads:
+                k.last_loads()
+                k.last_loads = None
             k.buf[tag + "x", "s"][...] = narrow_pair(kv_pair(t, tag, counts))
             k.send(tag + "x", k.buf[tag + "x", "s"], k.buf[tag + "x", "r"], k.dev_x())
 

time: 94.1 us -> 94 us (level)
  no operation moved by 1% of the time
where the time goes in v6:
time: 94 us; the launch traced here: 93.9 us
  Pallas kernels  93.1 us (99%)
    pallas_call x1, Pallas kernels, shards(): pl.pallas_call(functools.partial(kernel, [node.name for node in order], m...  93.1 us

profile of v6, /device:TPU:2, one launch (start us, length us, event | category | flops | bytes accessed | tf_op | source)
XLA Modules:
  0.0 93.9 jit_solution(11027887213197686007)
XLA Ops:
  0.0 93.1 %sublayer.1 = bf16[1024,256]{1,0:T(8,128)(2,1)S(1)} custom-call(s32[1,1024]{1,0:T(1,128)} %bitcast.1, bf16[1024,1024]{1,0:T(8,128)(2,1)} %refs_1_.1, bf16[1024,2048]{1,0:T(8,128)(2,1)} %refs_2_.1, bf16[1024,128]{1,0:T(8,128)(2,1)} %refs_3_.1, bf16[1024,128]{1,0:T(8,128)(2,1)} %refs_4_.1, bf16[2048,1024]{1,0:T(8,128)(2,1)} %refs_5_.1, ...), custom_call_target="tpu_custom_call" | custom-call | tf_op jit(solution)/shard_map/sublayer/pallas_call | solution.py:675
  93.2 0.8 copy.9

commit v7 on v5

--- a/solution.py
+++ b/solution.py
@@ -21,23 +21,23 @@
 R = ROWS // (2 * NZ)
 XFIRST = (((0, 768), (768, 640)), ((0, 640), (640, 640)))
 ZFIRST = (((1408, 640),), ((1280, 384), (1664, 384)))
-QUERY_PARTS = (2, 3, 0, 1)
+QUERY_PARTS = (2, 3, 1, 0)
 XWIDTH = tuple(sum(width for _, width in streams) for streams in XFIRST)
 OUTS = (((0,), (1,), (2,), (3,), (4,)), ((0,), (1,), (2,), (3,), (4,)))
 BF = jnp.bfloat16
 F32 = jnp.float32
 SCALE = math.log2(math.e) / math.sqrt(HEAD)
 ORDER = (
-    0, 9, 13, 1, 18, 5, 21, 135, 131, 3, 51, 6, 55, 10, 14, 56, 54, 140, 143, 19, 53, 22, 2, 132, 45, 4, 41, 52,
-    11, 144, 15, 71, 50, 7, 8, 66, 23, 57, 168, 42, 152, 46, 20, 12, 133, 24, 136, 145, 58, 141, 62, 82, 16, 43,
-    67, 25, 69, 72, 47, 166, 73, 165, 68, 59, 150, 154, 17, 149, 167, 30, 70, 27, 170, 74, 77, 63, 169, 26, 172,
-    171, 34, 151, 38, 176, 142, 155, 28, 153, 31, 156, 44, 78, 137, 134, 146, 173, 75, 35, 160, 60, 39, 32, 29, 79,
-    181, 161, 177, 48, 157, 174, 76, 40, 80, 36, 147, 64, 33, 61, 138, 81, 37, 178, 162, 158, 85, 175, 65, 49, 83,
-    84, 179, 139, 97, 107, 159, 182, 93, 110, 148, 163, 183, 180, 185, 217, 214, 111, 108, 164, 94, 184, 200, 100,
-    203, 98, 117, 121, 114, 86, 104, 90, 218, 215, 112, 186, 221, 224, 204, 95, 101, 109, 99, 201, 105, 210, 193,
-    196, 190, 87, 207, 115, 91, 219, 187, 225, 205, 216, 113, 96, 118, 102, 123, 197, 106, 202, 116, 191, 119, 194,
-    208, 211, 88, 92, 222, 230, 220, 122, 188, 223, 206, 226, 228, 198, 212, 209, 125, 195, 120, 192, 103, 89, 127,
-    189, 227, 213, 232, 199, 234, 129, 236, 233, 229, 126, 124, 235, 128, 231, 130, 237,
+    0, 13, 9, 1, 21, 18, 2, 41, 45, 4, 72, 66, 10, 6, 14, 22, 69, 70, 67, 5, 135, 143, 140, 68, 19, 3, 131, 52, 53,
+    73, 11, 23, 7, 150, 46, 50, 71, 15, 42, 82, 136, 20, 12, 24, 77, 141, 144, 47, 132, 43, 16, 8, 165, 152, 25,
+    156, 142, 51, 55, 78, 54, 166, 56, 168, 74, 154, 17, 57, 30, 58, 145, 26, 34, 27, 133, 169, 38, 137, 149, 62,
+    181, 59, 167, 153, 31, 155, 79, 35, 151, 160, 170, 39, 44, 146, 171, 75, 63, 134, 172, 176, 32, 60, 80, 28,
+    173, 161, 36, 61, 76, 64, 48, 157, 177, 29, 174, 33, 138, 40, 162, 81, 37, 147, 158, 65, 178, 84, 85, 49, 83,
+    139, 175, 179, 163, 110, 107, 148, 97, 93, 183, 159, 182, 180, 185, 217, 94, 100, 214, 164, 184, 203, 98, 111,
+    117, 104, 200, 108, 186, 196, 114, 218, 224, 121, 86, 204, 90, 190, 193, 228, 112, 215, 201, 95, 210, 118, 207,
+    99, 109, 221, 219, 115, 187, 205, 87, 101, 197, 211, 105, 91, 194, 225, 216, 202, 122, 113, 208, 96, 222, 106,
+    191, 123, 188, 220, 206, 119, 102, 116, 198, 88, 230, 92, 226, 212, 125, 223, 195, 192, 209, 232, 227, 213,
+    189, 103, 229, 199, 120, 89, 127, 124, 234, 231, 236, 129, 233, 126, 235, 237, 128, 130,
 )
 
 

time: 94.1 us -> 93.4 us (level)
  no operation moved by 1% of the time
where the time goes in v7:
time: 93.4 us; the launch traced here: 93.3 us
  Pallas kernels  92.5 us (99%)
    pallas_call x1, Pallas kernels, shards(): pl.pallas_call(functools.partial(kernel, [node.name for node in order], m...  92.5 us

profile of v7, /device:TPU:2, one launch (start us, length us, event | category | flops | bytes accessed | tf_op | source)
XLA Modules:
  0.0 93.3 jit_solution(10801938999326310553)
XLA Ops:
  0.0 92.5 %sublayer.1 = bf16[1024,256]{1,0:T(8,128)(2,1)S(1)} custom-call(s32[1,1024]{1,0:T(1,128)} %bitcast.1, bf16[1024,1024]{1,0:T(8,128)(2,1)} %refs_1_.1, bf16[1024,2048]{1,0:T(8,128)(2,1)} %refs_2_.1, bf16[1024,128]{1,0:T(8,128)(2,1)} %refs_3_.1, bf16[1024,128]{1,0:T(8,128)(2,1)} %refs_4_.1, bf16[2048,1024]{1,0:T(8,128)(2,1)} %refs_5_.1, ...), custom_call_target="tpu_custom_call" | custom-call | tf_op jit(solution)/shard_map/sublayer/pallas_call | solution.py:675
  92.5 0.8 copy.9
